TPU v7x, 512 devices: a whole 4x8x8 slice. The times are simulated.
512 devices in a mesh: rep: 32 (over z_hi, x, core), seq: 16 (over y, z_lo).
Axes of the slice: x: 4, y: 8, z: 8 (z_hi: 4, z_lo: 2; z = z_hi * 2 + z_lo), core: 2. Of those that a mesh axis runs over, the one named last changes fastest.
Arguments:
- queries: bfloat16 [32, 896, 2560], P('rep', 'seq'), may hold values from -130 to 130
- keys: bfloat16 [32, 896, 2560], P('rep', 'seq'), may hold values from -4 to 4
- values: bfloat16 [32, 896, 2560], P('rep', 'seq'), may hold values from -8 to 8
- residual: bfloat16 [32, 896, 5120], P('rep', None, 'seq'), may hold values from -3 to 3
- wo_values: bfloat16 [2, 2560, 5120], P(None, 'rep', 'seq'), may hold values from -0.0625 to 0.0625
- wo_exponents: int32 [2, 20, 40], replicated, may hold values from -1 to 2
- modulation: float32 [2, 5120], P(None, 'seq'), may hold values from 0.5 to 1.5
- expert_choice: int32 [32], replicated, may hold values from 0 to 1
- step_index: int32 [32], replicated, may hold values from 0 to 9
- lengths: int32 [32], replicated, may hold values from 224 to 896, as said below
Outputs:
- mixed: bfloat16 [32, 896, 5120], P('rep', None, 'seq')
Inputs may be any that keep to these rules, and one draw needn't show every extreme that they name: `lengths`: every clip has at least 224 valid tokens, and some clip has all 896.
All inputs are finite; a program needn't handle non-finite values.
Results may differ from a plain program's by a relative error of at most 0.008.
Values may be sent and summed in bfloat16 or wider, within the bound.
A program may use at most 64 MiB of HBM per device.

v0:
```python
import math

import jax
import jax.numpy as jnp
from jax import lax
from jax.sharding import PartitionSpec as P

D = 5120
HEADS = 20
HEAD_DIM = 128
BLOCK = 128
STEPS = 10


def from_behind(value, axis, steps):
    count = lax.axis_size(axis)
    pairs = [(source, (source + steps) % count) for source in range(count)]
    return lax.ppermute(value, axis, pairs)


def time_features(step_now, columns):
    half = D // 2
    offset = (columns % half).astype(jnp.float32)
    freq = jnp.exp(-math.log(10000.0) * offset / half)
    moment = 1000.0 * (1.0 - step_now.astype(jnp.float32) / STEPS)
    angle = moment * freq
    return jnp.where(columns < half, jnp.cos(angle), jnp.sin(angle))


def local(
    queries,
    keys,
    values,
    residual,
    wo_values,
    wo_exponents,
    modulation,
    expert_choice,
    step_index,
    lengths,
):
    tok_rows = queries.shape[1]
    width = queries.shape[2]
    col_count = residual.shape[2]
    cycle_size = lax.axis_size("seq")
    cycle_pos = lax.axis_index("seq")
    group = lax.axis_index("rep")
    group_ids = jnp.arange(expert_choice.shape[0], dtype=jnp.int32)
    expert = jnp.sum(jnp.where(group_ids == group, expert_choice, 0))
    step_now = jnp.sum(jnp.where(group_ids == group, step_index, 0))
    length = jnp.sum(jnp.where(group_ids == group, lengths, 0))
    query = queries[0].reshape(tok_rows, HEADS, HEAD_DIM)
    inv_root = HEAD_DIM ** (-0.5)

    def absorb(carry, pieces, first_row):
        key_rows, value_rows = pieces
        count = key_rows.shape[0]
        key_heads = key_rows.reshape(count, HEADS, HEAD_DIM)
        value_heads = value_rows.reshape(count, HEADS, HEAD_DIM)
        scores = (
            jnp.einsum("qhd,khd->hqk", query, key_heads, preferred_element_type=jnp.float32)
            * inv_root
        )
        valid = (first_row + jnp.arange(count) < length)[None, None, :]
        scores = jnp.where(valid, scores, -1e30)
        top_run, total_run, summed = carry
        top_new = jnp.maximum(top_run, jnp.max(scores, axis=-1))
        probs = jnp.where(valid, jnp.exp(scores - top_new[..., None]), 0.0)
        factor = jnp.exp(top_run - top_new)
        total_new = total_run * factor + jnp.sum(probs, axis=-1)
        update = jnp.einsum(
            "hqk,khd->hqd",
            probs.astype(jnp.bfloat16),
            value_heads,
            preferred_element_type=jnp.float32,
        )
        return (top_new, total_new, summed * factor[..., None] + update)

    start_state = (
        jnp.full((HEADS, tok_rows), -1e30, jnp.float32),
        jnp.zeros((HEADS, tok_rows), jnp.float32),
        jnp.zeros((HEADS, tok_rows, HEAD_DIM), jnp.float32),
    )
    own_blocks = (keys[0], values[0])
    first_state = absorb(start_state, own_blocks, cycle_pos * tok_rows)

    def turn(turn_no, packed):
        blocks, current = packed
        blocks = from_behind((blocks[0], blocks[1]), "seq", 1)
        source = (cycle_pos - turn_no) % cycle_size
        return (blocks, absorb(current, blocks, source * tok_rows))

    final_pack = lax.fori_loop(1, cycle_size, turn, (own_blocks, first_state))
    state = final_pack[1]
    top_run, total_run, summed = state
    attended = (
        (summed / total_run[..., None])
        .transpose(1, 0, 2)
        .reshape(tok_rows, width)
        .astype(jnp.bfloat16)
    )
    both_rows = lax.all_gather(wo_values, "rep", axis=1, tiled=True)
    chosen = jnp.where(expert == 1, both_rows[1], both_rows[0])
    table = jnp.where(expert == 1, wo_exponents[1], wo_exponents[0])
    powers = jnp.left_shift(jnp.ones_like(table), table + 1).astype(jnp.float32) * 0.5
    row_scale = jnp.repeat(powers, BLOCK, axis=0)
    columns = cycle_pos * col_count + jnp.arange(col_count, dtype=jnp.int32)
    picker = (
        columns[None, :] // BLOCK == jnp.arange(powers.shape[1], dtype=jnp.int32)[:, None]
    ).astype(jnp.float32)
    scale = jnp.dot(row_scale, picker, precision=lax.Precision.HIGHEST)
    weight = (chosen.astype(jnp.float32) * scale).astype(jnp.bfloat16)
    proj = jnp.dot(
        lax.all_gather(attended, "seq", axis=0, tiled=True),
        weight,
        preferred_element_type=jnp.float32,
    )
    offset_row = jnp.where(expert == 1, modulation[1], modulation[0])
    gate = offset_row + time_features(step_now, columns)
    mixed = (residual[0].astype(jnp.float32) + gate[None, :] * proj).astype(jnp.bfloat16)
    return mixed[None]


def solution(mesh):
    placed = (
        P("rep", "seq", None),
        P("rep", "seq", None),
        P("rep", "seq", None),
        P("rep", None, "seq"),
        P(None, "rep", "seq"),
        P(),
        P(None, "seq"),
        P(),
        P(),
        P(),
    )
    return jax.shard_map(
        local, mesh=mesh, in_specs=placed, out_specs=P("rep", None, "seq"), check_vma=False
    )
```

profile of v0, /device:TPU:6, one launch (start us, length us, event | category | flops | bytes accessed | tf_op | source)
XLA Modules:
  0.0 414.6 jit_solution(16420972958606322526)
XLA Ops:
  12.6 255.9 %while.23 = (s32[]{:T(128)}, bf16[56,2560]{1,0:T(8,128)(2,1)S(1)}, bf16[56,2560]{1,0:T(8,128)(2,1)S(1)}, f32[20,56]{1,0:T(8,128)S(1)}, f32[20,56]{1,0:T(8,128)S(...) while((s32[]{:T(128)}, bf16[56,2560]{1,0:T(8,128)(2,1)S(1)}, ...), condition=%wide.region_8.9_spmd, body=%wide.region_5.8_spmd.sunk | while | flops 32966208 | bytes 6272578 | solution.py:93
  12.6 4.3 %collective-permute-start = (bf16[56,2560]{1,0:T(8,128)(2,1)S(1)}, bf16[56,2560]{1,0:T(8,128)(2,1)S(1)}, u32[]{:S(2)}, u32[]{:S(2)}) collective-permute-start(bf16[56,2560]{1,0:T(8,128)(2,1)S(1)} %get-tuple-element.346), channel_id=1, source_target_pairs={{0,1},{1,2},{2,3},{3,4},{4,5},{5,6},{6,7},{7,8},{8,9},{9,10},{10,1... | collective-permute-start | bytes 860168 | tf_op jit(solution)/shard_map/while/body/eval_jaxpr/ppermute | solution.py:18
  20.2 7.2 %collective-permute-done = bf16[56,2560]{1,0:T(8,128)(2,1)S(1)} collective-permute-done((bf16[56,2560]{1,0:T(8,128)(2,1)S(1)}, bf16[56,2560]{1,0:T(8,128)(2,1)S(1)}, u32[]{:S(2)}, u32[]{:S(2)}) %collective-permute-start) | collective-permute-done | bytes 286752 | tf_op jit(solution)/shard_map/while/body/eval_jaxpr/ppermute | solution.py:18
  28.0 4.8 %collective-permute-done.1 = bf16[56,2560]{1,0:T(8,128)(2,1)S(1)} collective-permute-done((bf16[56,2560]{1,0:T(8,128)(2,1)S(1)}, bf16[56,2560]{1,0:T(8,128)(2,1)S(1)}, u32[]{:S(2)}, u32[]{:S(2)}) %collective-permute-start.1) | collective-permute-done | bytes 286752 | tf_op jit(solution)/shard_map/while/body/eval_jaxpr/ppermute | solution.py:18
  38.3 10.2 %collective-permute-done = bf16[56,2560]{1,0:T(8,128)(2,1)S(1)} collective-permute-done((bf16[56,2560]{1,0:T(8,128)(2,1)S(1)}, bf16[56,2560]{1,0:T(8,128)(2,1)S(1)}, u32[]{:S(2)}, u32[]{:S(2)}) %collective-permute-start) | collective-permute-done | bytes 286752 | tf_op jit(solution)/shard_map/while/body/eval_jaxpr/ppermute | solution.py:18
  49.1 3.9 collective-permute-done.1
  58.1 9.3 %collective-permute-done = bf16[56,2560]{1,0:T(8,128)(2,1)S(1)} collective-permute-done((bf16[56,2560]{1,0:T(8,128)(2,1)S(1)}, bf16[56,2560]{1,0:T(8,128)(2,1)S(1)}, u32[]{:S(2)}, u32[]{:S(2)}) %collective-permute-start) | collective-permute-done | bytes 286752 | tf_op jit(solution)/shard_map/while/body/eval_jaxpr/ppermute | solution.py:18
  76.0 8.8 %collective-permute-done = bf16[56,2560]{1,0:T(8,128)(2,1)S(1)} collective-permute-done((bf16[56,2560]{1,0:T(8,128)(2,1)S(1)}, bf16[56,2560]{1,0:T(8,128)(2,1)S(1)}, u32[]{:S(2)}, u32[]{:S(2)}) %collective-permute-start) | collective-permute-done | bytes 286752 | tf_op jit(solution)/shard_map/while/body/eval_jaxpr/ppermute | solution.py:18
  85.3 4.8 %collective-permute-done.1 = bf16[56,2560]{1,0:T(8,128)(2,1)S(1)} collective-permute-done((bf16[56,2560]{1,0:T(8,128)(2,1)S(1)}, bf16[56,2560]{1,0:T(8,128)(2,1)S(1)}, u32[]{:S(2)}, u32[]{:S(2)}) %collective-permute-start.1) | collective-permute-done | bytes 286752 | tf_op jit(solution)/shard_map/while/body/eval_jaxpr/ppermute | solution.py:18
  90.7 4.4 %collective-permute-start = (bf16[56,2560]{1,0:T(8,128)(2,1)S(1)}, bf16[56,2560]{1,0:T(8,128)(2,1)S(1)}, u32[]{:S(2)}, u32[]{:S(2)}) collective-permute-start(bf16[56,2560]{1,0:T(8,128)(2,1)S(1)} %get-tuple-element.346), channel_id=1, source_target_pairs={{0,1},{1,2},{2,3},{3,4},{4,5},{5,6},{6,7},{7,8},{8,9},{9,10},{10,1... | collective-permute-start | bytes 860168 | tf_op jit(solution)/shard_map/while/body/eval_jaxpr/ppermute | solution.py:18
  97.8 7.7 %collective-permute-done = bf16[56,2560]{1,0:T(8,128)(2,1)S(1)} collective-permute-done((bf16[56,2560]{1,0:T(8,128)(2,1)S(1)}, bf16[56,2560]{1,0:T(8,128)(2,1)S(1)}, u32[]{:S(2)}, u32[]{:S(2)}) %collective-permute-start) | collective-permute-done | bytes 286752 | tf_op jit(solution)/shard_map/while/body/eval_jaxpr/ppermute | solution.py:18
  109.2 3.4 collective-permute-start
  115.2 6.2 %collective-permute-done = bf16[56,2560]{1,0:T(8,128)(2,1)S(1)} collective-permute-done((bf16[56,2560]{1,0:T(8,128)(2,1)S(1)}, bf16[56,2560]{1,0:T(8,128)(2,1)S(1)}, u32[]{:S(2)}, u32[]{:S(2)}) %collective-permute-start) | collective-permute-done | bytes 286752 | tf_op jit(solution)/shard_map/while/body/eval_jaxpr/ppermute | solution.py:18
  125.1 4.4 %collective-permute-start = (bf16[56,2560]{1,0:T(8,128)(2,1)S(1)}, bf16[56,2560]{1,0:T(8,128)(2,1)S(1)}, u32[]{:S(2)}, u32[]{:S(2)}) collective-permute-start(bf16[56,2560]{1,0:T(8,128)(2,1)S(1)} %get-tuple-element.346), channel_id=1, source_target_pairs={{0,1},{1,2},{2,3},{3,4},{4,5},{5,6},{6,7},{7,8},{8,9},{9,10},{10,1... | collective-permute-start | bytes 860168 | tf_op jit(solution)/shard_map/while/body/eval_jaxpr/ppermute | solution.py:18
  133.3 5.9 %collective-permute-done = bf16[56,2560]{1,0:T(8,128)(2,1)S(1)} collective-permute-done((bf16[56,2560]{1,0:T(8,128)(2,1)S(1)}, bf16[56,2560]{1,0:T(8,128)(2,1)S(1)}, u32[]{:S(2)}, u32[]{:S(2)}) %collective-permute-start) | collective-permute-done | bytes 286752 | tf_op jit(solution)/shard_map/while/body/eval_jaxpr/ppermute | solution.py:18
  139.7 4.1 collective-permute-done.1
  146.3 4.5 %collective-permute-start.1 = (bf16[56,2560]{1,0:T(8,128)(2,1)S(1)}, bf16[56,2560]{1,0:T(8,128)(2,1)S(1)}, u32[]{:S(2)}, u32[]{:S(2)}) collective-permute-start(bf16[56,2560]{1,0:T(8,128)(2,1)S(1)} %get-tuple-element.347), channel_id=1, source_target_pairs={{0,1},{1,2},{2,3},{3,4},{4,5},{5,6},{6,7},{7,8},{8,9},{9,10},{10,1... | collective-permute-start | bytes 860168 | tf_op jit(solution)/shard_map/while/body/eval_jaxpr/ppermute | solution.py:18
  151.6 6.6 %collective-permute-done = bf16[56,2560]{1,0:T(8,128)(2,1)S(1)} collective-permute-done((bf16[56,2560]{1,0:T(8,128)(2,1)S(1)}, bf16[56,2560]{1,0:T(8,128)(2,1)S(1)}, u32[]{:S(2)}, u32[]{:S(2)}) %collective-permute-start) | collective-permute-done | bytes 286752 | tf_op jit(solution)/shard_map/while/body/eval_jaxpr/ppermute | solution.py:18
  164.4 3.9 collective-permute-start.1
  169.0 6.9 %collective-permute-done = bf16[56,2560]{1,0:T(8,128)(2,1)S(1)} collective-permute-done((bf16[56,2560]{1,0:T(8,128)(2,1)S(1)}, bf16[56,2560]{1,0:T(8,128)(2,1)S(1)}, u32[]{:S(2)}, u32[]{:S(2)}) %collective-permute-start) | collective-permute-done | bytes 286752 | tf_op jit(solution)/shard_map/while/body/eval_jaxpr/ppermute | solution.py:18
  181.5 3.2 collective-permute-start.1
  185.4 6.7 %collective-permute-done = bf16[56,2560]{1,0:T(8,128)(2,1)S(1)} collective-permute-done((bf16[56,2560]{1,0:T(8,128)(2,1)S(1)}, bf16[56,2560]{1,0:T(8,128)(2,1)S(1)}, u32[]{:S(2)}, u32[]{:S(2)}) %collective-permute-start) | collective-permute-done | bytes 286752 | tf_op jit(solution)/shard_map/while/body/eval_jaxpr/ppermute | solution.py:18
  200.9 6.5 %collective-permute-done = bf16[56,2560]{1,0:T(8,128)(2,1)S(1)} collective-permute-done((bf16[56,2560]{1,0:T(8,128)(2,1)S(1)}, bf16[56,2560]{1,0:T(8,128)(2,1)S(1)}, u32[]{:S(2)}, u32[]{:S(2)}) %collective-permute-start) | collective-permute-done | bytes 286752 | tf_op jit(solution)/shard_map/while/body/eval_jaxpr/ppermute | solution.py:18
  216.1 5.5 %collective-permute-done = bf16[56,2560]{1,0:T(8,128)(2,1)S(1)} collective-permute-done((bf16[56,2560]{1,0:T(8,128)(2,1)S(1)}, bf16[56,2560]{1,0:T(8,128)(2,1)S(1)}, u32[]{:S(2)}, u32[]{:S(2)}) %collective-permute-start) | collective-permute-done | bytes 286752 | tf_op jit(solution)/shard_map/while/body/eval_jaxpr/ppermute | solution.py:18
  227.3 3.5 collective-permute-start.1
  231.6 4.4 %collective-permute-done = bf16[56,2560]{1,0:T(8,128)(2,1)S(1)} collective-permute-done((bf16[56,2560]{1,0:T(8,128)(2,1)S(1)}, bf16[56,2560]{1,0:T(8,128)(2,1)S(1)}, u32[]{:S(2)}, u32[]{:S(2)}) %collective-permute-start) | collective-permute-done | bytes 286752 | tf_op jit(solution)/shard_map/while/body/eval_jaxpr/ppermute | solution.py:18
  241.6 3.8 collective-permute-start.1
  246.2 4.2 %collective-permute-done = bf16[56,2560]{1,0:T(8,128)(2,1)S(1)} collective-permute-done((bf16[56,2560]{1,0:T(8,128)(2,1)S(1)}, bf16[56,2560]{1,0:T(8,128)(2,1)S(1)}, u32[]{:S(2)}, u32[]{:S(2)}) %collective-permute-start) | collective-permute-done | bytes 286752 | tf_op jit(solution)/shard_map/while/body/eval_jaxpr/ppermute | solution.py:18
  259.9 4.9 %collective-permute-done = bf16[56,2560]{1,0:T(8,128)(2,1)S(1)} collective-permute-done((bf16[56,2560]{1,0:T(8,128)(2,1)S(1)}, bf16[56,2560]{1,0:T(8,128)(2,1)S(1)}, u32[]{:S(2)}, u32[]{:S(2)}) %collective-permute-start) | collective-permute-done | bytes 286752 | tf_op jit(solution)/shard_map/while/body/eval_jaxpr/ppermute | solution.py:18
  271.7 4.1 fusion.12
  275.9 126.8 %all-gather.3.cloned.1.call-done = bf16[896,2560]{1,0:T(8,128)(2,1)} async-done(((bf16[56,2560]{1,0:T(8,128)(2,1)}), bf16[896,2560]{1,0:T(8,128)(2,1)}) %all-gather.3.cloned.1.call-update) | async-done | bytes 4587536 | tf_op jit(solution)/shard_map/all_gather | solution.py:114
  402.7 5.0 %fusion.16 = bf16[1,896,320]{1,2,0:T(8,128)(2,1)} fusion(bf16[896,2560]{1,0:T(8,128)(2,1)} %all-gather.3.cloned.1.call-done, bf16[2560,320]{1,0:T(8,128)(2,1)S(1)} %fusion.12, bf16[1,896,320]{1,2,0:T(8,128)(2,1)S(1)} %copy-done.4, f32[320]{0:T(512)S(1)} %fusion.37), kind=kOutput, calls=%fused_computation.24 | convolution fusion | flops 1469153280 | bytes 7374080 | tf_op jit(solution)/shard_map/dot_general | solution.py:113
  (204 shorter events, 108.2 us)
Async XLA Ops:
  6.5 265.1 %all-gather.5.cloned.1.call-start = ((), (), s32[]{:S(2)}) async-start(), calls=%async_computation.1 | async-start | bytes 4055040 | tf_op jit(solution)/shard_map/all_gather | solution.py:102
  8.5 394.2 %all-gather.3.cloned.1.call-start = ((), (), s32[]{:S(2)}) async-start(), calls=%async_computation | async-start | bytes 4874240 | tf_op jit(solution)/shard_map/all_gather | solution.py:114
  12.6 14.8 %collective-permute-start = (bf16[56,2560]{1,0:T(8,128)(2,1)S(1)}, bf16[56,2560]{1,0:T(8,128)(2,1)S(1)}, u32[]{:S(2)}, u32[]{:S(2)}) collective-permute-start(bf16[56,2560]{1,0:T(8,128)(2,1)S(1)} %get-tuple-element.346), channel_id=1, source_target_pairs={{0,1},{1,2},{2,3},{3,4},{4,5},{5,6},{6,7},{7,8},{8,9},{9,10},{10,1... | collective-permute-start | bytes 860168 | tf_op jit(solution)/shard_map/while/body/eval_jaxpr/ppermute | solution.py:18
  16.9 15.9 %collective-permute-start.1 = (bf16[56,2560]{1,0:T(8,128)(2,1)S(1)}, bf16[56,2560]{1,0:T(8,128)(2,1)S(1)}, u32[]{:S(2)}, u32[]{:S(2)}) collective-permute-start(bf16[56,2560]{1,0:T(8,128)(2,1)S(1)} %get-tuple-element.347), channel_id=1, source_target_pairs={{0,1},{1,2},{2,3},{3,4},{4,5},{5,6},{6,7},{7,8},{8,9},{9,10},{10,1... | collective-permute-start | bytes 860168 | tf_op jit(solution)/shard_map/while/body/eval_jaxpr/ppermute | solution.py:18
  33.3 15.2 %collective-permute-start = (bf16[56,2560]{1,0:T(8,128)(2,1)S(1)}, bf16[56,2560]{1,0:T(8,128)(2,1)S(1)}, u32[]{:S(2)}, u32[]{:S(2)}) collective-permute-start(bf16[56,2560]{1,0:T(8,128)(2,1)S(1)} %get-tuple-element.346), channel_id=1, source_target_pairs={{0,1},{1,2},{2,3},{3,4},{4,5},{5,6},{6,7},{7,8},{8,9},{9,10},{10,1... | collective-permute-start | bytes 860168 | tf_op jit(solution)/shard_map/while/body/eval_jaxpr/ppermute | solution.py:18
  35.3 17.7 %collective-permute-start.1 = (bf16[56,2560]{1,0:T(8,128)(2,1)S(1)}, bf16[56,2560]{1,0:T(8,128)(2,1)S(1)}, u32[]{:S(2)}, u32[]{:S(2)}) collective-permute-start(bf16[56,2560]{1,0:T(8,128)(2,1)S(1)} %get-tuple-element.347), channel_id=1, source_target_pairs={{0,1},{1,2},{2,3},{3,4},{4,5},{5,6},{6,7},{7,8},{8,9},{9,10},{10,1... | collective-permute-start | bytes 860168 | tf_op jit(solution)/shard_map/while/body/eval_jaxpr/ppermute | solution.py:18
  53.5 13.9 %collective-permute-start = (bf16[56,2560]{1,0:T(8,128)(2,1)S(1)}, bf16[56,2560]{1,0:T(8,128)(2,1)S(1)}, u32[]{:S(2)}, u32[]{:S(2)}) collective-permute-start(bf16[56,2560]{1,0:T(8,128)(2,1)S(1)} %get-tuple-element.346), channel_id=1, source_target_pairs={{0,1},{1,2},{2,3},{3,4},{4,5},{5,6},{6,7},{7,8},{8,9},{9,10},{10,1... | collective-permute-start | bytes 860168 | tf_op jit(solution)/shard_map/while/body/eval_jaxpr/ppermute | solution.py:18
  55.5 15.4 %collective-permute-start.1 = (bf16[56,2560]{1,0:T(8,128)(2,1)S(1)}, bf16[56,2560]{1,0:T(8,128)(2,1)S(1)}, u32[]{:S(2)}, u32[]{:S(2)}) collective-permute-start(bf16[56,2560]{1,0:T(8,128)(2,1)S(1)} %get-tuple-element.347), channel_id=1, source_target_pairs={{0,1},{1,2},{2,3},{3,4},{4,5},{5,6},{6,7},{7,8},{8,9},{9,10},{10,1... | collective-permute-start | bytes 860168 | tf_op jit(solution)/shard_map/while/body/eval_jaxpr/ppermute | solution.py:18
  71.4 13.3 %collective-permute-start = (bf16[56,2560]{1,0:T(8,128)(2,1)S(1)}, bf16[56,2560]{1,0:T(8,128)(2,1)S(1)}, u32[]{:S(2)}, u32[]{:S(2)}) collective-permute-start(bf16[56,2560]{1,0:T(8,128)(2,1)S(1)} %get-tuple-element.346), channel_id=1, source_target_pairs={{0,1},{1,2},{2,3},{3,4},{4,5},{5,6},{6,7},{7,8},{8,9},{9,10},{10,1... | collective-permute-start | bytes 860168 | tf_op jit(solution)/shard_map/while/body/eval_jaxpr/ppermute | solution.py:18
  73.4 16.7 %collective-permute-start.1 = (bf16[56,2560]{1,0:T(8,128)(2,1)S(1)}, bf16[56,2560]{1,0:T(8,128)(2,1)S(1)}, u32[]{:S(2)}, u32[]{:S(2)}) collective-permute-start(bf16[56,2560]{1,0:T(8,128)(2,1)S(1)} %get-tuple-element.347), channel_id=1, source_target_pairs={{0,1},{1,2},{2,3},{3,4},{4,5},{5,6},{6,7},{7,8},{8,9},{9,10},{10,1... | collective-permute-start | bytes 860168 | tf_op jit(solution)/shard_map/while/body/eval_jaxpr/ppermute | solution.py:18
  90.7 14.8 %collective-permute-start = (bf16[56,2560]{1,0:T(8,128)(2,1)S(1)}, bf16[56,2560]{1,0:T(8,128)(2,1)S(1)}, u32[]{:S(2)}, u32[]{:S(2)}) collective-permute-start(bf16[56,2560]{1,0:T(8,128)(2,1)S(1)} %get-tuple-element.346), channel_id=1, source_target_pairs={{0,1},{1,2},{2,3},{3,4},{4,5},{5,6},{6,7},{7,8},{8,9},{9,10},{10,1... | collective-permute-start | bytes 860168 | tf_op jit(solution)/shard_map/while/body/eval_jaxpr/ppermute | solution.py:18
  95.1 13.5 %collective-permute-start.1 = (bf16[56,2560]{1,0:T(8,128)(2,1)S(1)}, bf16[56,2560]{1,0:T(8,128)(2,1)S(1)}, u32[]{:S(2)}, u32[]{:S(2)}) collective-permute-start(bf16[56,2560]{1,0:T(8,128)(2,1)S(1)} %get-tuple-element.347), channel_id=1, source_target_pairs={{0,1},{1,2},{2,3},{3,4},{4,5},{5,6},{6,7},{7,8},{8,9},{9,10},{10,1... | collective-permute-start | bytes 860168 | tf_op jit(solution)/shard_map/while/body/eval_jaxpr/ppermute | solution.py:18
  109.2 12.2 %collective-permute-start = (bf16[56,2560]{1,0:T(8,128)(2,1)S(1)}, bf16[56,2560]{1,0:T(8,128)(2,1)S(1)}, u32[]{:S(2)}, u32[]{:S(2)}) collective-permute-start(bf16[56,2560]{1,0:T(8,128)(2,1)S(1)} %get-tuple-element.346), channel_id=1, source_target_pairs={{0,1},{1,2},{2,3},{3,4},{4,5},{5,6},{6,7},{7,8},{8,9},{9,10},{10,1... | collective-permute-start | bytes 860168 | tf_op jit(solution)/shard_map/while/body/eval_jaxpr/ppermute | solution.py:18
  112.6 11.9 %collective-permute-start.1 = (bf16[56,2560]{1,0:T(8,128)(2,1)S(1)}, bf16[56,2560]{1,0:T(8,128)(2,1)S(1)}, u32[]{:S(2)}, u32[]{:S(2)}) collective-permute-start(bf16[56,2560]{1,0:T(8,128)(2,1)S(1)} %get-tuple-element.347), channel_id=1, source_target_pairs={{0,1},{1,2},{2,3},{3,4},{4,5},{5,6},{6,7},{7,8},{8,9},{9,10},{10,1... | collective-permute-start | bytes 860168 | tf_op jit(solution)/shard_map/while/body/eval_jaxpr/ppermute | solution.py:18
  125.1 14.1 %collective-permute-start = (bf16[56,2560]{1,0:T(8,128)(2,1)S(1)}, bf16[56,2560]{1,0:T(8,128)(2,1)S(1)}, u32[]{:S(2)}, u32[]{:S(2)}) collective-permute-start(bf16[56,2560]{1,0:T(8,128)(2,1)S(1)} %get-tuple-element.346), channel_id=1, source_target_pairs={{0,1},{1,2},{2,3},{3,4},{4,5},{5,6},{6,7},{7,8},{8,9},{9,10},{10,1... | collective-permute-start | bytes 860168 | tf_op jit(solution)/shard_map/while/body/eval_jaxpr/ppermute | solution.py:18
  129.5 14.3 %collective-permute-start.1 = (bf16[56,2560]{1,0:T(8,128)(2,1)S(1)}, bf16[56,2560]{1,0:T(8,128)(2,1)S(1)}, u32[]{:S(2)}, u32[]{:S(2)}) collective-permute-start(bf16[56,2560]{1,0:T(8,128)(2,1)S(1)} %get-tuple-element.347), channel_id=1, source_target_pairs={{0,1},{1,2},{2,3},{3,4},{4,5},{5,6},{6,7},{7,8},{8,9},{9,10},{10,1... | collective-permute-start | bytes 860168 | tf_op jit(solution)/shard_map/while/body/eval_jaxpr/ppermute | solution.py:18
  144.4 13.8 %collective-permute-start = (bf16[56,2560]{1,0:T(8,128)(2,1)S(1)}, bf16[56,2560]{1,0:T(8,128)(2,1)S(1)}, u32[]{:S(2)}, u32[]{:S(2)}) collective-permute-start(bf16[56,2560]{1,0:T(8,128)(2,1)S(1)} %get-tuple-element.346), channel_id=1, source_target_pairs={{0,1},{1,2},{2,3},{3,4},{4,5},{5,6},{6,7},{7,8},{8,9},{9,10},{10,1... | collective-permute-start | bytes 860168 | tf_op jit(solution)/shard_map/while/body/eval_jaxpr/ppermute | solution.py:18
  146.3 15.5 %collective-permute-start.1 = (bf16[56,2560]{1,0:T(8,128)(2,1)S(1)}, bf16[56,2560]{1,0:T(8,128)(2,1)S(1)}, u32[]{:S(2)}, u32[]{:S(2)}) collective-permute-start(bf16[56,2560]{1,0:T(8,128)(2,1)S(1)} %get-tuple-element.347), channel_id=1, source_target_pairs={{0,1},{1,2},{2,3},{3,4},{4,5},{5,6},{6,7},{7,8},{8,9},{9,10},{10,1... | collective-permute-start | bytes 860168 | tf_op jit(solution)/shard_map/while/body/eval_jaxpr/ppermute | solution.py:18
  162.4 13.4 %collective-permute-start = (bf16[56,2560]{1,0:T(8,128)(2,1)S(1)}, bf16[56,2560]{1,0:T(8,128)(2,1)S(1)}, u32[]{:S(2)}, u32[]{:S(2)}) collective-permute-start(bf16[56,2560]{1,0:T(8,128)(2,1)S(1)} %get-tuple-element.346), channel_id=1, source_target_pairs={{0,1},{1,2},{2,3},{3,4},{4,5},{5,6},{6,7},{7,8},{8,9},{9,10},{10,1... | collective-permute-start | bytes 860168 | tf_op jit(solution)/shard_map/while/body/eval_jaxpr/ppermute | solution.py:18
  164.4 14.6 %collective-permute-start.1 = (bf16[56,2560]{1,0:T(8,128)(2,1)S(1)}, bf16[56,2560]{1,0:T(8,128)(2,1)S(1)}, u32[]{:S(2)}, u32[]{:S(2)}) collective-permute-start(bf16[56,2560]{1,0:T(8,128)(2,1)S(1)} %get-tuple-element.347), channel_id=1, source_target_pairs={{0,1},{1,2},{2,3},{3,4},{4,5},{5,6},{6,7},{7,8},{8,9},{9,10},{10,1... | collective-permute-start | bytes 860168 | tf_op jit(solution)/shard_map/while/body/eval_jaxpr/ppermute | solution.py:18
  179.6 12.5 %collective-permute-start = (bf16[56,2560]{1,0:T(8,128)(2,1)S(1)}, bf16[56,2560]{1,0:T(8,128)(2,1)S(1)}, u32[]{:S(2)}, u32[]{:S(2)}) collective-permute-start(bf16[56,2560]{1,0:T(8,128)(2,1)S(1)} %get-tuple-element.346), channel_id=1, source_target_pairs={{0,1},{1,2},{2,3},{3,4},{4,5},{5,6},{6,7},{7,8},{8,9},{9,10},{10,1... | collective-permute-start | bytes 860168 | tf_op jit(solution)/shard_map/while/body/eval_jaxpr/ppermute | solution.py:18
  181.5 13.7 %collective-permute-start.1 = (bf16[56,2560]{1,0:T(8,128)(2,1)S(1)}, bf16[56,2560]{1,0:T(8,128)(2,1)S(1)}, u32[]{:S(2)}, u32[]{:S(2)}) collective-permute-start(bf16[56,2560]{1,0:T(8,128)(2,1)S(1)} %get-tuple-element.347), channel_id=1, source_target_pairs={{0,1},{1,2},{2,3},{3,4},{4,5},{5,6},{6,7},{7,8},{8,9},{9,10},{10,1... | collective-permute-start | bytes 860168 | tf_op jit(solution)/shard_map/while/body/eval_jaxpr/ppermute | solution.py:18
  195.8 11.6 %collective-permute-start = (bf16[56,2560]{1,0:T(8,128)(2,1)S(1)}, bf16[56,2560]{1,0:T(8,128)(2,1)S(1)}, u32[]{:S(2)}, u32[]{:S(2)}) collective-permute-start(bf16[56,2560]{1,0:T(8,128)(2,1)S(1)} %get-tuple-element.346), channel_id=1, source_target_pairs={{0,1},{1,2},{2,3},{3,4},{4,5},{5,6},{6,7},{7,8},{8,9},{9,10},{10,1... | collective-permute-start | bytes 860168 | tf_op jit(solution)/shard_map/while/body/eval_jaxpr/ppermute | solution.py:18
  197.7 12.7 %collective-permute-start.1 = (bf16[56,2560]{1,0:T(8,128)(2,1)S(1)}, bf16[56,2560]{1,0:T(8,128)(2,1)S(1)}, u32[]{:S(2)}, u32[]{:S(2)}) collective-permute-start(bf16[56,2560]{1,0:T(8,128)(2,1)S(1)} %get-tuple-element.347), channel_id=1, source_target_pairs={{0,1},{1,2},{2,3},{3,4},{4,5},{5,6},{6,7},{7,8},{8,9},{9,10},{10,1... | collective-permute-start | bytes 860168 | tf_op jit(solution)/shard_map/while/body/eval_jaxpr/ppermute | solution.py:18
  211.0 10.7 %collective-permute-start = (bf16[56,2560]{1,0:T(8,128)(2,1)S(1)}, bf16[56,2560]{1,0:T(8,128)(2,1)S(1)}, u32[]{:S(2)}, u32[]{:S(2)}) collective-permute-start(bf16[56,2560]{1,0:T(8,128)(2,1)S(1)} %get-tuple-element.346), channel_id=1, source_target_pairs={{0,1},{1,2},{2,3},{3,4},{4,5},{5,6},{6,7},{7,8},{8,9},{9,10},{10,1... | collective-permute-start | bytes 860168 | tf_op jit(solution)/shard_map/while/body/eval_jaxpr/ppermute | solution.py:18
  213.0 11.8 %collective-permute-start.1 = (bf16[56,2560]{1,0:T(8,128)(2,1)S(1)}, bf16[56,2560]{1,0:T(8,128)(2,1)S(1)}, u32[]{:S(2)}, u32[]{:S(2)}) collective-permute-start(bf16[56,2560]{1,0:T(8,128)(2,1)S(1)} %get-tuple-element.347), channel_id=1, source_target_pairs={{0,1},{1,2},{2,3},{3,4},{4,5},{5,6},{6,7},{7,8},{8,9},{9,10},{10,1... | collective-permute-start | bytes 860168 | tf_op jit(solution)/shard_map/while/body/eval_jaxpr/ppermute | solution.py:18
  225.4 10.6 %collective-permute-start = (bf16[56,2560]{1,0:T(8,128)(2,1)S(1)}, bf16[56,2560]{1,0:T(8,128)(2,1)S(1)}, u32[]{:S(2)}, u32[]{:S(2)}) collective-permute-start(bf16[56,2560]{1,0:T(8,128)(2,1)S(1)} %get-tuple-element.346), channel_id=1, source_target_pairs={{0,1},{1,2},{2,3},{3,4},{4,5},{5,6},{6,7},{7,8},{8,9},{9,10},{10,1... | collective-permute-start | bytes 860168 | tf_op jit(solution)/shard_map/while/body/eval_jaxpr/ppermute | solution.py:18
  227.3 11.8 %collective-permute-start.1 = (bf16[56,2560]{1,0:T(8,128)(2,1)S(1)}, bf16[56,2560]{1,0:T(8,128)(2,1)S(1)}, u32[]{:S(2)}, u32[]{:S(2)}) collective-permute-start(bf16[56,2560]{1,0:T(8,128)(2,1)S(1)} %get-tuple-element.347), channel_id=1, source_target_pairs={{0,1},{1,2},{2,3},{3,4},{4,5},{5,6},{6,7},{7,8},{8,9},{9,10},{10,1... | collective-permute-start | bytes 860168 | tf_op jit(solution)/shard_map/while/body/eval_jaxpr/ppermute | solution.py:18
  239.7 10.6 %collective-permute-start = (bf16[56,2560]{1,0:T(8,128)(2,1)S(1)}, bf16[56,2560]{1,0:T(8,128)(2,1)S(1)}, u32[]{:S(2)}, u32[]{:S(2)}) collective-permute-start(bf16[56,2560]{1,0:T(8,128)(2,1)S(1)} %get-tuple-element.346), channel_id=1, source_target_pairs={{0,1},{1,2},{2,3},{3,4},{4,5},{5,6},{6,7},{7,8},{8,9},{9,10},{10,1... | collective-permute-start | bytes 860168 | tf_op jit(solution)/shard_map/while/body/eval_jaxpr/ppermute | solution.py:18
  241.6 11.9 %collective-permute-start.1 = (bf16[56,2560]{1,0:T(8,128)(2,1)S(1)}, bf16[56,2560]{1,0:T(8,128)(2,1)S(1)}, u32[]{:S(2)}, u32[]{:S(2)}) collective-permute-start(bf16[56,2560]{1,0:T(8,128)(2,1)S(1)} %get-tuple-element.347), channel_id=1, source_target_pairs={{0,1},{1,2},{2,3},{3,4},{4,5},{5,6},{6,7},{7,8},{8,9},{9,10},{10,1... | collective-permute-start | bytes 860168 | tf_op jit(solution)/shard_map/while/body/eval_jaxpr/ppermute | solution.py:18
  254.1 10.6 %collective-permute-start = (bf16[56,2560]{1,0:T(8,128)(2,1)S(1)}, bf16[56,2560]{1,0:T(8,128)(2,1)S(1)}, u32[]{:S(2)}, u32[]{:S(2)}) collective-permute-start(bf16[56,2560]{1,0:T(8,128)(2,1)S(1)} %get-tuple-element.346), channel_id=1, source_target_pairs={{0,1},{1,2},{2,3},{3,4},{4,5},{5,6},{6,7},{7,8},{8,9},{9,10},{10,1... | collective-permute-start | bytes 860168 | tf_op jit(solution)/shard_map/while/body/eval_jaxpr/ppermute | solution.py:18
  256.0 11.8 %collective-permute-start.1 = (bf16[56,2560]{1,0:T(8,128)(2,1)S(1)}, bf16[56,2560]{1,0:T(8,128)(2,1)S(1)}, u32[]{:S(2)}, u32[]{:S(2)}) collective-permute-start(bf16[56,2560]{1,0:T(8,128)(2,1)S(1)} %get-tuple-element.347), channel_id=1, source_target_pairs={{0,1},{1,2},{2,3},{3,4},{4,5},{5,6},{6,7},{7,8},{8,9},{9,10},{10,1... | collective-permute-start | bytes 860168 | tf_op jit(solution)/shard_map/while/body/eval_jaxpr/ppermute | solution.py:18
  (6 other events, 912.6 us)
Sparse Core Ops, SparseCore 0:
  10.6 96.1 all-gather.4
  269.5 133.1 all-gather.2
where the time goes:
time: 416 us; the launch traced here: 415 us
  waiting for transfers between devices  274 us (66%)
  starting transfers between devices  80.3 us (19%)
  matrix products  23 us (6%)
  other arithmetic  16.3 us (4%)
  between operations  14.9 us (4%)
  local copies, waits for them, and re-layouts  4.28 us (1%)
    ppermute x30, waiting for transfers between devices, from_behind(): return lax.ppermute(value, axis, pairs)  147 us
    all_gather x1, waiting for transfers between devices, local(): lax.all_gather(attended, 'seq', axis=0, tiled=True)  127 us
    ppermute x30, starting transfers between devices, from_behind(): return lax.ppermute(value, axis, pairs)  80.2 us
    lt x16, other arithmetic, absorb(): valid = (first_row + jnp.arange(count) < length)[None, None, :]  11.1 us
    dot_general x16, matrix products, absorb(): jnp.einsum('hqk,khd->hqd', probs.astype(jnp.bfloat16), value_heads, prefe...  8.97 us
  transfers between devices with their start and end apart: 32, of which 31 were waited for; matrix products, arithmetic and copies ran while one was open for 9% of the time, Pallas kernels for 0%

commit v1 on v0

v1 whole, which is shorter than its diff:
```python
import math

import jax
import jax.numpy as jnp
import numpy as np
from jax import lax
from jax.experimental import pallas as pl
from jax.experimental.pallas import tpu as pltpu
from jax.sharding import PartitionSpec as P

D = 5120
HEADS = 20
HEAD_DIM = 128
STEPS = 10
NY = 8
NZL = 2
NX = 4
NZH = 4
NZ = NZL * NZH
ROWS = 56
SEQ = ROWS * NY * NZL
CLIPS = 2 * NX * NZH
HALF = ROWS * NY
QUART = HALF // 2
COLS = 320
DEPTH = 80
SCALE = HEAD_DIM**-0.5 * math.log2(math.e)

MESH = pl.DeviceIdType.MESH
F32 = jnp.float32
BF16 = jnp.bfloat16


def mod(value, size):
    return lax.rem(value + size, size)


def kernel(
    q_ref,
    k_ref,
    v_ref,
    res_ref,
    wo_ref,
    exps_hbm,
    mod_hbm,
    freq_hbm,
    expert_hbm,
    step_hbm,
    len_hbm,
    out_ref,
    exps_ref,
    mod_ref,
    freq_ref,
    expert_ref,
    step_ref,
    len_ref,
    pre,
    qkv,
    stage,
    wbuf,
    wo_rows,
    wch,
    dstage,
    attm,
    acc,
    psend,
    precv,
    resv,
    nat,
    stab,
    bias_ref,
    gate_ref,
    loc_sem,
    small_sem,
    as_sem,
    ar_sem,
    sr_sem,
    fs_sem,
    ks_sem,
    kr_sem,
    zs_sem,
    zr_sem,
    xs_sem,
    xr_sem,
    rs_sem,
    rr_sem,
    ds_sem,
    dr_sem,
    gs_sem,
    gr_sem,
    os_sem,
    or_sem,
):
    rep = lax.axis_index("rep")
    seq = lax.axis_index("seq")
    c = lax.rem(rep, 2)
    x = lax.rem(rep // 2, NX)
    zh = rep // (2 * NX)
    y = seq // NZL
    zl = lax.rem(seq, NZL)
    z = zh * NZL + zl

    def dev_y(yy):
        return {"rep": rep, "seq": yy * NZL + zl}

    def dev_z(zz):
        return {"rep": (zz // NZL) * (2 * NX) + x * 2 + c, "seq": y * NZL + lax.rem(zz, NZL)}

    def dev_x(xx):
        return {"rep": zh * (2 * NX) + xx * 2 + c, "seq": seq}

    partner = {"rep": rep, "seq": y * NZL + 1 - zl}
    sibling = {"rep": rep + 1 - 2 * c, "seq": seq}
    z_next, z_prev = dev_z(mod(z + 1, NZ)), dev_z(mod(z - 1, NZ))
    x_next, x_prev = dev_x(mod(x + 1, NX)), dev_x(mod(x - 1, NX))
    y_next, y_prev = dev_y(mod(y + 1, NY)), dev_y(mod(y - 1, NY))

    def send(src, dst, ss, rs, dev):
        pltpu.make_async_remote_copy(
            src_ref=src, dst_ref=dst, send_sem=ss, recv_sem=rs, device_id=dev, device_id_type=MESH
        ).start()

    def wait(ref, sem):
        pltpu.make_async_copy(ref, ref, sem).wait()

    def wslot(zz, xx):
        return wbuf.at[lax.rem(zz, NZL), :, zz // NZL, pl.ds((xx * 2 + c) * DEPTH, DEPTH), :]

    def lanes(phase, n):
        return pl.ds(0, HEAD_DIM) if phase == 0 else pl.ds(HEAD_DIM, (n - 1) * HEAD_DIM)

    def columns(yy, phase, n):
        first = (yy // 2) * 5 + (0 if n == 3 else 3) + phase
        return pl.ds(pl.multiple_of(first * HEAD_DIM, HEAD_DIM), HEAD_DIM if phase == 0 else (n - 1) * HEAD_DIM)

    small = (
        (exps_hbm, exps_ref),
        (expert_hbm, expert_ref),
        (step_hbm, step_ref),
        (len_hbm, len_ref),
        (mod_hbm, mod_ref),
        (freq_hbm.at[seq], freq_ref),
    )
    pltpu.make_async_copy(wo_ref, wo_rows, loc_sem.at[3]).start()
    for index, (source, target) in enumerate(small):
        pltpu.make_async_copy(source, target, small_sem.at[index]).start()

    barrier = pltpu.get_barrier_semaphore()
    for d in (1, 2, 3, 5, 6, 7):
        pl.semaphore_signal(barrier, inc=1, device_id=dev_y(mod(y + d, NY)), device_id_type=MESH)
    for dev in (z_next, z_prev, x_next, x_prev, sibling):
        pl.semaphore_signal(barrier, inc=1, device_id=dev, device_id_type=MESH)

    for j, ref in enumerate((q_ref, k_ref, v_ref)):
        pltpu.make_async_copy(ref.at[0], pre.at[j], loc_sem.at[j]).start()
    pltpu.make_async_copy(res_ref, resv, loc_sem.at[4]).start()
    own_w = wslot(z, x)
    twice = 2 - 4 * c
    mid_to, mid_from = mod(y + twice, NY), mod(y - twice, NY)

    for index, (source, target) in enumerate(small):
        pltpu.make_async_copy(source, target, small_sem.at[index]).wait()
    expert, expert_beside = expert_ref[rep], expert_ref[rep + 1 - 2 * c]
    for choice in range(2):
        powers = (jnp.left_shift(jnp.ones((HEADS, D // 128), jnp.int32), exps_ref[:, choice, :] + 1).astype(F32) * 0.5).astype(BF16)
        column = seq * COLS + lax.broadcasted_iota(jnp.int32, (D // 128, COLS), 1)
        hot = (column // 128 == lax.broadcasted_iota(jnp.int32, (D // 128, COLS), 0)).astype(F32).astype(BF16)
        stab[choice] = jnp.dot(powers, hot, preferred_element_type=F32)
    wait(wo_rows, loc_sem.at[3])
    for choice in range(2):
        for piece in range(DEPTH // 16):
            head = (rep * DEPTH + piece * 16) // HEAD_DIM
            rows = wo_rows[choice, piece * 16 : (piece + 1) * 16, :].astype(F32) * stab[choice, pl.ds(head, 1), :]
            place = pl.multiple_of((x * 2 + c) * DEPTH + piece * 16, 16)
            wbuf[zl, choice, zh, pl.ds(place, 16), :] = rows.astype(BF16)

    flat = lax.broadcasted_iota(jnp.int32, (1, SEQ), 1)
    upper = (flat >= HALF).astype(jnp.int32)
    within = flat - upper * HALF
    source = sum((within >= ROWS * m).astype(jnp.int32) for m in range(1, NY))
    position = within + (source + upper) * ROWS
    bias_ref[...] = jnp.where(position < len_ref[rep], 0.0, -1e30)
    angle = 1000.0 * (1.0 - step_ref[rep].astype(F32) / STEPS) * freq_ref[...]
    feature = jnp.where(seq < NY * NZL // 2, jnp.cos(angle), jnp.sin(angle))
    gate_ref[...] = mod_ref[pl.ds(expert, 1), :] + feature
    pl.semaphore_wait(barrier, 11)

    def run(n):
        def heads(d):
            return n if d % 2 == 0 else 5 - n

        def a2a(d, phase):
            to = mod(y + d, NY)
            cut = lanes(phase, heads(d))
            source = pre.at[:, :, columns(to, phase, heads(d))]
            if d == NY // 2:
                send(source, stage.at[:, :, cut], as_sem.at[phase, d], sr_sem.at[phase], dev_y(mid_to))
            else:
                send(source, qkv.at[:, zl, y, :, cut], as_sem.at[phase, d], ar_sem.at[phase, d], dev_y(to))

        def own_kv(phase):
            source = pre.at[pl.ds(1, 2), :, columns(y, phase, n)]
            target = qkv.at[pl.ds(1, 2), zl, y, :, lanes(phase, n)]
            send(source, target, ks_sem.at[phase, y], kr_sem.at[phase, y], partner)

        def mid_tick(phase):
            block = stage.at[:, :, lanes(phase, n)]
            wait(block, sr_sem.at[phase])
            target = qkv.at[:, zl, mid_from, :, lanes(phase, n)]
            send(block, target, fs_sem.at[phase], ar_sem.at[phase, NY // 2], dev_y(mid_to))

        def kv_tick(d, phase):
            source = mod(y - d, NY)
            wait(qkv.at[:, zl, source, :, lanes(phase, n)], ar_sem.at[phase, d])
            block = qkv.at[pl.ds(1, 2), zl, source, :, lanes(phase, n)]
            send(block, block, ks_sem.at[phase, source], kr_sem.at[phase, source], partner)

        def kv_done(phase):
            for source in range(NY):
                wait(qkv.at[pl.ds(1, 2), 1 - zl, source, :, lanes(phase, n)], kr_sem.at[phase, source])

        def z_tick(d):
            block = wslot(mod(z - d, NZ), x)
            wait(block, zr_sem.at[d])
            if d < NZ // 2:
                send(block, block, zs_sem.at[0, d], zr_sem.at[d + 1], z_next)
            elif d > NZ // 2 + 1:
                send(block, block, zs_sem.at[1, d], zr_sem.at[d - 1], z_prev)
            send(block, block, xs_sem.at[0, d], xr_sem.at[0, d], x_next)
            send(block, block, xs_sem.at[1, d], xr_sem.at[1, d], x_prev)

        def x_tick(d):
            zz = mod(z - d, NZ)
            left, right = wslot(zz, mod(x - 1, NX)), wslot(zz, mod(x + 1, NX))
            wait(left, xr_sem.at[0, d])
            wait(right, xr_sem.at[1, d])
            if d < NZ // 2:
                send(left, left, rs_sem.at[d], rr_sem.at[d], x_next)
            else:
                send(right, right, rs_sem.at[d], rr_sem.at[d], x_prev)

        def die_push(xx, index):
            rows = pl.ds(pl.multiple_of((xx * 2 + c) * DEPTH, 16), DEPTH)
            for place in range(NZL):
                for group in range(NZH):
                    low, high = wbuf[place, 0, group, rows, :], wbuf[place, 1, group, rows, :]
                    wch[place, group, rows, :] = jnp.where(expert == 1, high, low)
                    dstage[index, place, group] = jnp.where(expert_beside == 1, high, low)
            send(dstage.at[index], wch.at[:, :, rows, :], ds_sem.at[index], dr_sem.at[index], sibling)

        def head_rows(stream, j):
            rows = qkv[stream, :, :, :, j * HEAD_DIM : (j + 1) * HEAD_DIM].astype(F32)
            return rows.reshape(SEQ, HEAD_DIM).astype(BF16)

        def attend(j, half, keys, values):
            first = half * (NY // 2)
            query = qkv[0, zl, pl.ds(first, NY // 2), :, j * HEAD_DIM : (j + 1) * HEAD_DIM]
            query = query.astype(F32).reshape(QUART, HEAD_DIM).astype(BF16)
            scores = lax.dot_general(query, keys, (((1,), (1,)), ((), ())), preferred_element_type=F32)
            scores = scores + bias_ref[...]
            top = jnp.max(scores, axis=1, keepdims=True)
            probs = jnp.exp2((scores - top) * SCALE)
            total = jnp.sum(probs, axis=1, keepdims=True)
            summed = jnp.dot(probs.astype(BF16), values, preferred_element_type=F32)
            attm[y, half * QUART : (half + 1) * QUART, j * HEAD_DIM : (j + 1) * HEAD_DIM] = (summed / total).astype(BF16)

        def region(yy, kind, count):
            if kind == 0:
                return attm.at[yy, :, pl.ds(0, HEAD_DIM)]
            if kind in (1, 2):
                return attm.at[yy, pl.ds((kind - 1) * QUART, QUART), pl.ds(HEAD_DIM, (count - 1) * HEAD_DIM)]
            return attm.at[yy, pl.ds(0, QUART), pl.ds((kind - 2) * HEAD_DIM, HEAD_DIM)]

        def ring_send(t, direction, kind, yy):
            block = region(yy, kind, heads(t - 1))
            sems = gs_sem.at[direction, t - 1, kind], gr_sem.at[direction, t - 1, kind]
            send(block, block, *sems, (y_next, y_prev)[direction])

        def ring_wait(t, direction, kind):
            yy = mod(y - t if direction == 0 else y + t, NY)
            wait(region(yy, kind, heads(t)), gr_sem.at[direction, t - 1, kind])
            return yy

        def ring_tick(t, kind):
            for direction in range(2):
                yy = ring_wait(t, direction, kind)
                if t < NY // 2 - 1:
                    ring_send(t + 1, direction, kind, yy)
                else:
                    for last_kind in last_kinds(direction, heads(t)):
                        if last_kind == kind or (kind == 1 and last_kind in (3, 4)):
                            ring_send(t + 1, direction, last_kind, yy)

        def last_kinds(direction, count):
            if direction == 1:
                return (3, 2)
            return (0, 4) if count == 3 else (0,)

        def project(yy, count, which, rows=slice(0, HALF), fresh=False):
            first = 0 if count == 3 else 3 * HEAD_DIM
            weight = wch[zl if which == 0 else 1 - zl, yy // 2, first : first + count * HEAD_DIM, :]
            made = jnp.dot(attm[yy, rows, : count * HEAD_DIM], weight, preferred_element_type=F32)
            if fresh:
                acc[which, rows] = made
            else:
                acc[which, rows] += made

        def project_two(first, step, which):
            def one(i, _):
                project(mod(y + first + step * i, NY), heads(first), which)
                return 0

            lax.fori_loop(0, 2, one, 0)

        send(own_w, own_w, zs_sem.at[0, 0], zr_sem.at[1], z_next)
        send(own_w, own_w, zs_sem.at[1, 0], zr_sem.at[NZ - 1], z_prev)
        for j in range(3):
            wait(pre.at[j], loc_sem.at[j])
        for d in (4, 3, 5, 2, 6, 1, 7):
            a2a(d, 0)
        own_kv(0)
        send(own_w, own_w, xs_sem.at[0, 0], xr_sem.at[0, 0], x_next)
        send(own_w, own_w, xs_sem.at[1, 0], xr_sem.at[1, 0], x_prev)
        start = pl.multiple_of(((y // 2) * 5 + (0 if n == 3 else 3)) * HEAD_DIM, HEAD_DIM)
        own_block = qkv.at[:, zl, y, :, pl.ds(0, n * HEAD_DIM)]
        pltpu.make_async_copy(pre.at[:, :, pl.ds(start, n * HEAD_DIM)], own_block, loc_sem.at[5]).start()
        mid_tick(0)
        for d in (4, 3, 5):
            a2a(d, 1)
        z_tick(1)
        z_tick(7)
        x_tick(0)
        for d in (2, 6, 1, 7):
            a2a(d, 1)
        own_kv(1)
        for d in (1, 7, 2, 6, 3, 5, 4):
            kv_tick(d, 0)
        z_tick(2)
        z_tick(6)
        mid_tick(1)

        wait(own_block, loc_sem.at[5])
        kv_done(0)
        keys, values = head_rows(1, 0), head_rows(2, 0)
        for half in range(2):
            attend(0, half, keys, values)
        ring_send(1, 0, 0, y)
        ring_send(1, 1, 0, y)
        x_tick(1)
        x_tick(7)
        z_tick(3)
        z_tick(5)
        kv_tick(1, 1)
        kv_tick(7, 1)
        kv_tick(2, 1)
        kv_tick(6, 1)
        z_tick(4)
        kv_tick(3, 1)
        kv_tick(5, 1)
        kv_tick(4, 1)
        die_push(x, 0)
        ring_tick(1, 0)

        kv_done(1)
        pairs = {j: (head_rows(1, j), head_rows(2, j)) for j in range(1, n)}
        for j in range(1, n):
            attend(j, 0, *pairs[j])
        ring_send(1, 0, 1, y)
        ring_send(1, 1, 1, y)
        ring_tick(2, 0)
        x_tick(2)
        x_tick(6)
        for j in range(1, n):
            attend(j, 1, *pairs[j])
        ring_send(1, 0, 2, y)
        ring_send(1, 1, 2, y)
        x_tick(3)
        x_tick(5)
        ring_tick(1, 1)
        ring_tick(3, 0)
        ring_tick(1, 2)
        x_tick(4)
        die_push(mod(x - 1, NX), 1)
        die_push(mod(x + 1, NX), 2)
        ring_tick(2, 1)
        ring_tick(2, 2)
        far = mod(x + 2, NX)
        for d in range(NZ):
            wait(wslot(mod(z - d, NZ), far), rr_sem.at[d])
        die_push(far, 3)
        ring_tick(3, 1)
        ring_tick(3, 2)
        for index, xx in enumerate((x, mod(x - 1, NX), mod(x + 1, NX), far)):
            wait(wch.at[:, :, pl.ds((xx * 2 + 1 - c) * DEPTH, DEPTH), :], dr_sem.at[index])
        project(y, n, 1, fresh=True)
        project_two(1, 6, 1)
        project_two(2, 4, 1)
        project_two(3, 2, 1)
        project(y, n, 0, fresh=True)
        project_two(1, 6, 0)

        last = mod(y + NY // 2, NY)
        for kind in last_kinds(0, n):
            ring_wait(NY // 2, 0, kind)
        for half in range(2):
            ring_wait(NY // 2, 1, (3, 2)[half])
            rows = slice(half * QUART, (half + 1) * QUART)
            project(last, n, 1, rows)
            psend[rows] = acc[1, rows].astype(BF16)
            send(psend.at[rows], precv.at[rows], os_sem.at[half], or_sem.at[half], partner)
        project_two(2, 4, 0)
        project_two(3, 2, 0)
        project(last, n, 0)

        for phase in range(2):
            for d in range(1, NY):
                wait(qkv.at[:, zl, y, :, lanes(phase, heads(d))], as_sem.at[phase, d])
            wait(stage.at[:, :, lanes(phase, n)], fs_sem.at[phase])
            for source in range(NY):
                wait(qkv.at[pl.ds(1, 2), zl, source, :, lanes(phase, n)], ks_sem.at[phase, source])
        for t in range(1, NY // 2 + 1):
            for direction in range(2):
                for kind in (0, 1, 2) if t < NY // 2 else last_kinds(direction, heads(t - 1)):
                    wait(region(y, kind, heads(t - 1)), gs_sem.at[direction, t - 1, kind])

    pl.when(lax.rem(y, 2) == 0)(lambda: run(3))
    pl.when(lax.rem(y, 2) == 1)(lambda: run(2))

    for d in (0, 1, 2, 3):
        wait(own_w, zs_sem.at[0, d])
    for d in (0, 7, 6):
        wait(own_w, zs_sem.at[1, d])
    for d in range(NZ):
        wait(own_w, xs_sem.at[0, d])
        wait(own_w, xs_sem.at[1, d])
        wait(own_w, rs_sem.at[d])
    for index in range(NX):
        wait(dstage.at[index], ds_sem.at[index])
    wait(resv, loc_sem.at[4])
    gate = gate_ref[...]
    for block in range(NY):
        nat[pl.ds((block * NZL + zl) * ROWS, ROWS), :] = acc[0, block * ROWS : (block + 1) * ROWS] * gate
    for half in range(2):
        rows = slice(half * QUART, (half + 1) * QUART)
        wait(precv.at[rows], or_sem.at[half])
        acc[1, rows] = precv[rows].astype(F32)
        for block in range(half * NY // 2, (half + 1) * NY // 2):
            nat[pl.ds((block * NZL + 1 - zl) * ROWS, ROWS), :] = acc[1, block * ROWS : (block + 1) * ROWS] * gate
        for block in ((0, 1, 2), (3, 4, 5, 6))[half]:
            tokens = slice(block * 128, (block + 1) * 128)
            out_ref[0, :, tokens] = (resv[0, :, tokens].astype(F32) + nat[tokens, :].T).astype(BF16)
    for half in range(2):
        wait(psend.at[half * QUART : (half + 1) * QUART], os_sem.at[half])


def local(queries, keys, values, residual, wo_values, wo_exponents, modulation, expert_choice, step_index, lengths):
    offset = np.arange(D) % (D // 2)
    freq = np.exp(-math.log(10000.0) * offset / (D // 2)).astype(np.float32).reshape(D // COLS, 1, COLS)
    hbm = pl.BlockSpec(memory_space=pl.ANY)
    vmem = pl.BlockSpec(memory_space=pltpu.VMEM)
    dma = pltpu.SemaphoreType.DMA
    mixed = pl.pallas_call(
        kernel,
        out_shape=pltpu.VMEM((1, COLS, SEQ), BF16),
        in_specs=[hbm] * 11,
        out_specs=vmem,
        scratch_shapes=[
            pltpu.VMEM((HEADS, 2, D // 128), jnp.int32),
            pltpu.VMEM((2, COLS), F32),
            pltpu.VMEM((1, COLS), F32),
            pltpu.SMEM((CLIPS,), jnp.int32),
            pltpu.SMEM((CLIPS,), jnp.int32),
            pltpu.SMEM((CLIPS,), jnp.int32),
            pltpu.VMEM((3, ROWS, HEADS * HEAD_DIM), BF16),
            pltpu.VMEM((3, NZL, NY, ROWS, 3 * HEAD_DIM), BF16),
            pltpu.VMEM((3, ROWS, 3 * HEAD_DIM), BF16),
            pltpu.VMEM((NZL, 2, NZH, 2 * NX * DEPTH, COLS), BF16),
            pltpu.VMEM((2, DEPTH, COLS), BF16),
            pltpu.VMEM((NZL, NZH, 2 * NX * DEPTH, COLS), BF16),
            pltpu.VMEM((NX, NZL, NZH, DEPTH, COLS), BF16),
            pltpu.VMEM((NY, HALF, 3 * HEAD_DIM), BF16),
            pltpu.VMEM((2, HALF, COLS), F32),
            pltpu.VMEM((HALF, COLS), BF16),
            pltpu.VMEM((HALF, COLS), BF16),
            pltpu.VMEM((1, COLS, SEQ), BF16),
            pltpu.VMEM((SEQ, COLS), F32),
            pltpu.VMEM((2, HEADS, COLS), F32),
            pltpu.VMEM((1, SEQ), F32),
            pltpu.VMEM((1, COLS), F32),
            dma((6,)),
            dma((6,)),
            dma((2, NY)),
            dma((2, NY)),
            dma((2,)),
            dma((2,)),
            dma((2, NY)),
            dma((2, NY)),
            dma((2, NZ)),
            dma((NZ,)),
            dma((2, NZ)),
            dma((2, NZ)),
            dma((NZ,)),
            dma((NZ,)),
            dma((NX,)),
            dma((NX,)),
            dma((2, NY // 2, 5)),
            dma((2, NY // 2, 5)),
            dma((2,)),
            dma((2,)),
        ],
        compiler_params=pltpu.CompilerParams(
            collective_id=0, has_side_effects=True, vmem_limit_bytes=62 * 2**20
        ),
        cost_estimate=pl.CostEstimate(flops=2 * 10**9, bytes_accessed=3 * 10**6, transcendentals=10**6),
    )(
        queries,
        keys,
        values,
        jnp.swapaxes(residual, 1, 2),
        wo_values,
        jnp.swapaxes(wo_exponents, 0, 1),
        modulation,
        jnp.asarray(freq),
        expert_choice,
        step_index,
        lengths,
    )
    return jnp.swapaxes(mixed, 1, 2)


def solution(mesh):
    placed = (
        P("rep", "seq", None),
        P("rep", "seq", None),
        P("rep", "seq", None),
        P("rep", None, "seq"),
        P(None, "rep", "seq"),
        P(),
        P(None, "seq"),
        P(),
        P(),
        P(),
    )
    return jax.shard_map(
        local, mesh=mesh, in_specs=placed, out_specs=P("rep", None, "seq"), check_vma=False
    )
```

time: 416 us -> 77.6 us (0.19)
  the two profiles are of different devices: /device:TPU:6 before, /device:TPU:8 now
where the time goes in v1:
time: 77.6 us; the launch traced here: 77.5 us
  Pallas kernels  76.7 us (99%)
  local copies, waits for them, and re-layouts  0.81 us (1%)
    pallas_call x1, Pallas kernels, local(): pl.pallas_call(kernel, out_shape=pltpu.VMEM((1, COLS, SEQ), BF16), in_spe...  76.7 us

profile of v1, /device:TPU:8, one launch (start us, length us, event | category | flops | bytes accessed | tf_op | source)
XLA Modules:
  0.0 77.5 jit_solution(72635972152185034)
XLA Ops:
  0.0 76.7 %shard_map.109 = bf16[1,320,896]{2,1,0:T(8,128)(2,1)S(1)} custom-call(bf16[1,56,2560]{2,1,0:T(8,128)(2,1)} %q_ref.1, bf16[1,56,2560]{2,1,0:T(8,128)(2,1)} %k_ref.1, bf16[1,56,2560]{2,1,0:T(8,128)(2,1)} %v_ref.1, bf16[1,320,896]{2,1,0:T(8,128)(2,1)} %bitcast.4, bf16[2,80,320]{2,1,0:T(8,128)(2,1)} %wo_ref.1, s32[20,2,40]{2,1,0:T(2,128)} %bitcast.5, ...), custom_call_target="tpu_custom_call" | custom-call | flops 2000000000 | bytes 3000000 | tf_op jit(solution)/shard_map/pallas_call | solution.py:462
  76.7 0.8 %copy.13 = bf16[1,896,320]{1,2,0:T(8,128)(2,1)} copy(bf16[1,896,320]{1,2,0:T(8,128)(2,1)S(1)} %bitcast.3) | data formatting | bytes 1146880

commit v2 on v1

--- a/solution.py
+++ b/solution.py
@@ -23,9 +23,13 @@
 HALF = ROWS * NY
 QUART = HALF // 2
 COLS = 320
+MAIN = 256
+EDGE = COLS - MAIN
+PACK = 2 * COLS
 DEPTH = 80
 SCALE = HEAD_DIM**-0.5 * math.log2(math.e)
 
+OWN, OTHER, EDGES = 0, 1, 2
 MESH = pl.DeviceIdType.MESH
 F32 = jnp.float32
 BF16 = jnp.bfloat16
@@ -56,15 +60,17 @@
     len_ref,
     pre,
     qkv,
-    stage,
     wbuf,
     wo_rows,
     wch,
     dstage,
     attm,
     acc,
+    edge,
     psend,
     precv,
+    esend,
+    erecv,
     resv,
     nat,
     stab,
@@ -74,8 +80,6 @@
     small_sem,
     as_sem,
     ar_sem,
-    sr_sem,
-    fs_sem,
     ks_sem,
     kr_sem,
     zs_sem,
@@ -124,7 +128,7 @@
         pltpu.make_async_copy(ref, ref, sem).wait()
 
     def wslot(zz, xx):
-        return wbuf.at[lax.rem(zz, NZL), :, zz // NZL, pl.ds((xx * 2 + c) * DEPTH, DEPTH), :]
+        return wbuf.at[lax.rem(zz, NZL), zz // NZL, pl.ds((xx * 2 + c) * DEPTH, DEPTH), :]
 
     def lanes(phase, n):
         return pl.ds(0, HEAD_DIM) if phase == 0 else pl.ds(HEAD_DIM, (n - 1) * HEAD_DIM)
@@ -146,7 +150,7 @@
         pltpu.make_async_copy(source, target, small_sem.at[index]).start()
 
     barrier = pltpu.get_barrier_semaphore()
-    for d in (1, 2, 3, 5, 6, 7):
+    for d in range(1, NY):
         pl.semaphore_signal(barrier, inc=1, device_id=dev_y(mod(y + d, NY)), device_id_type=MESH)
     for dev in (z_next, z_prev, x_next, x_prev, sibling):
         pl.semaphore_signal(barrier, inc=1, device_id=dev, device_id_type=MESH)
@@ -155,12 +159,9 @@
         pltpu.make_async_copy(ref.at[0], pre.at[j], loc_sem.at[j]).start()
     pltpu.make_async_copy(res_ref, resv, loc_sem.at[4]).start()
     own_w = wslot(z, x)
-    twice = 2 - 4 * c
-    mid_to, mid_from = mod(y + twice, NY), mod(y - twice, NY)
 
     for index, (source, target) in enumerate(small):
         pltpu.make_async_copy(source, target, small_sem.at[index]).wait()
-    expert, expert_beside = expert_ref[rep], expert_ref[rep + 1 - 2 * c]
     for choice in range(2):
         powers = (jnp.left_shift(jnp.ones((HEADS, D // 128), jnp.int32), exps_ref[:, choice, :] + 1).astype(F32) * 0.5).astype(BF16)
         column = seq * COLS + lax.broadcasted_iota(jnp.int32, (D // 128, COLS), 1)
@@ -171,19 +172,29 @@
         for piece in range(DEPTH // 16):
             head = (rep * DEPTH + piece * 16) // HEAD_DIM
             rows = wo_rows[choice, piece * 16 : (piece + 1) * 16, :].astype(F32) * stab[choice, pl.ds(head, 1), :]
-            place = pl.multiple_of((x * 2 + c) * DEPTH + piece * 16, 16)
-            wbuf[zl, choice, zh, pl.ds(place, 16), :] = rows.astype(BF16)
-
-    flat = lax.broadcasted_iota(jnp.int32, (1, SEQ), 1)
-    upper = (flat >= HALF).astype(jnp.int32)
-    within = flat - upper * HALF
-    source = sum((within >= ROWS * m).astype(jnp.int32) for m in range(1, NY))
-    position = within + (source + upper) * ROWS
-    bias_ref[...] = jnp.where(position < len_ref[rep], 0.0, -1e30)
-    angle = 1000.0 * (1.0 - step_ref[rep].astype(F32) / STEPS) * freq_ref[...]
-    feature = jnp.where(seq < NY * NZL // 2, jnp.cos(angle), jnp.sin(angle))
-    gate_ref[...] = mod_ref[pl.ds(expert, 1), :] + feature
-    pl.semaphore_wait(barrier, 11)
+            wo_rows[choice, piece * 16 : (piece + 1) * 16, :] = rows.astype(BF16)
+    packed = jnp.zeros((DEPTH, PACK), F32)
+    origin = lax.broadcasted_iota(jnp.int32, (COLS, PACK), 0)
+    lane = lax.broadcasted_iota(jnp.int32, (COLS, PACK), 1)
+    for choice in range(2):
+        low = jnp.where(origin < MAIN, choice * MAIN + origin, 2 * MAIN + choice * EDGE + origin - MAIN)
+        high = jnp.where(origin < EDGE, 2 * MAIN + (1 - choice) * EDGE + origin, choice * MAIN + origin - EDGE)
+        hot = (lane == jnp.where(zl == 0, low, high)).astype(F32).astype(BF16)
+        packed += jnp.dot(wo_rows[choice], hot, preferred_element_type=F32)
+    wbuf[zl, zh, pl.ds(pl.multiple_of((x * 2 + c) * DEPTH, 16), DEPTH), :] = packed.astype(BF16)
+    pl.semaphore_wait(barrier, 12)
+
+    def tables():
+        flat = lax.broadcasted_iota(jnp.int32, (1, SEQ), 1)
+        upper = (flat >= HALF).astype(jnp.int32)
+        within = flat - upper * HALF
+        source = sum((within >= ROWS * m).astype(jnp.int32) for m in range(1, NY))
+        position = within + (source + upper) * ROWS
+        bias_ref[...] = jnp.where(position < len_ref[rep], 0.0, -1e30)
+        angle = 1000.0 * (1.0 - step_ref[rep].astype(F32) / STEPS) * freq_ref[...]
+        feature = jnp.where(seq < NY * NZL // 2, jnp.cos(angle), jnp.sin(angle))
+        gate = mod_ref[pl.ds(expert_ref[rep], 1), :] + feature
+        gate_ref[...] = jnp.broadcast_to(gate, (128, COLS)).T
 
     def run(n):
         def heads(d):
@@ -193,21 +204,12 @@
             to = mod(y + d, NY)
             cut = lanes(phase, heads(d))
             source = pre.at[:, :, columns(to, phase, heads(d))]
-            if d == NY // 2:
-                send(source, stage.at[:, :, cut], as_sem.at[phase, d], sr_sem.at[phase], dev_y(mid_to))
-            else:
-                send(source, qkv.at[:, zl, y, :, cut], as_sem.at[phase, d], ar_sem.at[phase, d], dev_y(to))
+            send(source, qkv.at[:, zl, y, :, cut], as_sem.at[phase, d], ar_sem.at[phase, d], dev_y(to))
 
         def own_kv(phase):
             source = pre.at[pl.ds(1, 2), :, columns(y, phase, n)]
             target = qkv.at[pl.ds(1, 2), zl, y, :, lanes(phase, n)]
             send(source, target, ks_sem.at[phase, y], kr_sem.at[phase, y], partner)
-
-        def mid_tick(phase):
-            block = stage.at[:, :, lanes(phase, n)]
-            wait(block, sr_sem.at[phase])
-            target = qkv.at[:, zl, mid_from, :, lanes(phase, n)]
-            send(block, target, fs_sem.at[phase], ar_sem.at[phase, NY // 2], dev_y(mid_to))
 
         def kv_tick(d, phase):
             source = mod(y - d, NY)
@@ -241,12 +243,20 @@
 
         def die_push(xx, index):
             rows = pl.ds(pl.multiple_of((xx * 2 + c) * DEPTH, 16), DEPTH)
-            for place in range(NZL):
-                for group in range(NZH):
-                    low, high = wbuf[place, 0, group, rows, :], wbuf[place, 1, group, rows, :]
-                    wch[place, group, rows, :] = jnp.where(expert == 1, high, low)
-                    dstage[index, place, group] = jnp.where(expert_beside == 1, high, low)
-            send(dstage.at[index], wch.at[:, :, rows, :], ds_sem.at[index], dr_sem.at[index], sibling)
+            expert, expert_beside = expert_ref[rep], expert_ref[rep + 1 - 2 * c]
+            left = lax.broadcasted_iota(jnp.int32, (DEPTH, 2 * EDGE), 1) < EDGE
+            for group in range(NZH):
+                for place in range(NZL):
+                    low, high = wbuf[place, group, rows, :MAIN], wbuf[place, group, rows, MAIN : 2 * MAIN]
+                    cut = slice(place * MAIN, (place + 1) * MAIN)
+                    wch[group, rows, cut] = jnp.where(expert == 1, high, low)
+                    dstage[index, group, :, cut] = jnp.where(expert_beside == 1, high, low)
+                edges = [wbuf[place, group, rows, 2 * MAIN :].astype(F32) for place in range(NZL)]
+                low = jnp.where(left, edges[0], edges[1]).astype(BF16)
+                high = jnp.where(left, edges[1], edges[0]).astype(BF16)
+                wch[group, rows, 2 * MAIN :] = jnp.where(expert == 1, high, low)
+                dstage[index, group, :, 2 * MAIN :] = jnp.where(expert_beside == 1, high, low)
+            send(dstage.at[index], wch.at[:, rows, :], ds_sem.at[index], dr_sem.at[index], sibling)
 
         def head_rows(stream, j):
             rows = qkv[stream, :, :, :, j * HEAD_DIM : (j + 1) * HEAD_DIM].astype(F32)
@@ -296,18 +306,23 @@
                 return (3, 2)
             return (0, 4) if count == 3 else (0,)
 
-        def project(yy, count, which, rows=slice(0, HALF), fresh=False):
+        def project(yy, count, part, rows=slice(0, HALF), fresh=False):
             first = 0 if count == 3 else 3 * HEAD_DIM
-            weight = wch[zl if which == 0 else 1 - zl, yy // 2, first : first + count * HEAD_DIM, :]
+            if part == EDGES:
+                cut, total = pl.ds(2 * MAIN, 2 * EDGE), edge
+            else:
+                cut, total = pl.ds(pl.multiple_of((zl if part == OWN else 1 - zl) * MAIN, MAIN), MAIN), acc.at[part]
+            weight = wch[yy // 2, first : first + count * HEAD_DIM, cut]
             made = jnp.dot(attm[yy, rows, : count * HEAD_DIM], weight, preferred_element_type=F32)
             if fresh:
-                acc[which, rows] = made
+                total[rows] = made
             else:
-                acc[which, rows] += made
-
-        def project_two(first, step, which):
+                total[rows] += made
+
+        def project_two(first, step, *parts):
             def one(i, _):
-                project(mod(y + first + step * i, NY), heads(first), which)
+                for part in parts:
+                    project(mod(y + first + step * i, NY), heads(first), part)
                 return 0
 
             lax.fori_loop(0, 2, one, 0)
@@ -324,7 +339,7 @@
         start = pl.multiple_of(((y // 2) * 5 + (0 if n == 3 else 3)) * HEAD_DIM, HEAD_DIM)
         own_block = qkv.at[:, zl, y, :, pl.ds(0, n * HEAD_DIM)]
         pltpu.make_async_copy(pre.at[:, :, pl.ds(start, n * HEAD_DIM)], own_block, loc_sem.at[5]).start()
-        mid_tick(0)
+        tables()
         for d in (4, 3, 5):
             a2a(d, 1)
         z_tick(1)
@@ -337,7 +352,6 @@
             kv_tick(d, 0)
         z_tick(2)
         z_tick(6)
-        mid_tick(1)
 
         wait(own_block, loc_sem.at[5])
         kv_done(0)
@@ -358,6 +372,8 @@
         kv_tick(3, 1)
         kv_tick(5, 1)
         kv_tick(4, 1)
+        x_tick(2)
+        x_tick(6)
         die_push(x, 0)
         ring_tick(1, 0)
 
@@ -368,18 +384,16 @@
         ring_send(1, 0, 1, y)
         ring_send(1, 1, 1, y)
         ring_tick(2, 0)
-        x_tick(2)
-        x_tick(6)
+        x_tick(3)
+        x_tick(5)
         for j in range(1, n):
             attend(j, 1, *pairs[j])
         ring_send(1, 0, 2, y)
         ring_send(1, 1, 2, y)
-        x_tick(3)
-        x_tick(5)
         ring_tick(1, 1)
+        x_tick(4)
         ring_tick(3, 0)
         ring_tick(1, 2)
-        x_tick(4)
         die_push(mod(x - 1, NX), 1)
         die_push(mod(x + 1, NX), 2)
         ring_tick(2, 1)
@@ -391,31 +405,39 @@
         ring_tick(3, 1)
         ring_tick(3, 2)
         for index, xx in enumerate((x, mod(x - 1, NX), mod(x + 1, NX), far)):
-            wait(wch.at[:, :, pl.ds((xx * 2 + 1 - c) * DEPTH, DEPTH), :], dr_sem.at[index])
-        project(y, n, 1, fresh=True)
-        project_two(1, 6, 1)
-        project_two(2, 4, 1)
-        project_two(3, 2, 1)
-        project(y, n, 0, fresh=True)
-        project_two(1, 6, 0)
+            wait(wch.at[:, pl.ds((xx * 2 + 1 - c) * DEPTH, DEPTH), :], dr_sem.at[index])
+        project(y, n, OTHER, fresh=True)
+        project(y, n, EDGES, fresh=True)
+        project_two(1, 6, OTHER, EDGES)
+        project_two(2, 4, OTHER, EDGES)
+        project_two(3, 2, OTHER, EDGES)
+        project(y, n, OWN, fresh=True)
 
         last = mod(y + NY // 2, NY)
+        turned = lax.rem(expert_ref[rep] + zl, 2) * EDGE
+        left = lax.broadcasted_iota(jnp.int32, (QUART // 2, 2 * EDGE), 1) < EDGE
         for kind in last_kinds(0, n):
             ring_wait(NY // 2, 0, kind)
         for half in range(2):
             ring_wait(NY // 2, 1, (3, 2)[half])
             rows = slice(half * QUART, (half + 1) * QUART)
-            project(last, n, 1, rows)
-            psend[rows] = acc[1, rows].astype(BF16)
-            send(psend.at[rows], precv.at[rows], os_sem.at[half], or_sem.at[half], partner)
-        project_two(2, 4, 0)
-        project_two(3, 2, 0)
-        project(last, n, 0)
+            project(last, n, OTHER, rows)
+            psend[rows] = acc[OTHER, rows].astype(BF16)
+            send(psend.at[rows], precv.at[rows], os_sem.at[0, half], or_sem.at[0, half], partner)
+            project(last, n, EDGES, rows)
+            top = edge[half * QUART : half * QUART + QUART // 2]
+            low = edge[half * QUART + QUART // 2 : (half + 1) * QUART]
+            both = jnp.where(left, pltpu.roll(top, EDGE - turned, 1), pltpu.roll(low, turned, 1))
+            esend[half] = both.astype(BF16)
+            send(esend.at[half], erecv.at[half], os_sem.at[1, half], or_sem.at[1, half], partner)
+        project_two(1, 6, OWN)
+        project_two(2, 4, OWN)
+        project_two(3, 2, OWN)
+        project(last, n, OWN)
 
         for phase in range(2):
             for d in range(1, NY):
                 wait(qkv.at[:, zl, y, :, lanes(phase, heads(d))], as_sem.at[phase, d])
-            wait(stage.at[:, :, lanes(phase, n)], fs_sem.at[phase])
             for source in range(NY):
                 wait(qkv.at[pl.ds(1, 2), zl, source, :, lanes(phase, n)], ks_sem.at[phase, source])
         for t in range(1, NY // 2 + 1):
@@ -437,20 +459,34 @@
     for index in range(NX):
         wait(dstage.at[index], ds_sem.at[index])
     wait(resv, loc_sem.at[4])
-    gate = gate_ref[...]
+    turned = lax.rem(expert_ref[rep] + zl, 2) * EDGE
     for block in range(NY):
-        nat[pl.ds((block * NZL + zl) * ROWS, ROWS), :] = acc[0, block * ROWS : (block + 1) * ROWS] * gate
+        rows, place = slice(block * ROWS, (block + 1) * ROWS), pl.ds((block * NZL + zl) * ROWS, ROWS)
+        nat[place, :MAIN] = acc[OWN, rows]
+        nat[place, MAIN:] = pltpu.roll(edge[rows], turned, 1)
+    main_at = pl.ds(pl.multiple_of(zl * EDGE, EDGE), MAIN)
+    edge_at = pl.ds(pl.multiple_of((1 - zl) * MAIN, EDGE), EDGE)
     for half in range(2):
         rows = slice(half * QUART, (half + 1) * QUART)
-        wait(precv.at[rows], or_sem.at[half])
-        acc[1, rows] = precv[rows].astype(F32)
+        wait(precv.at[rows], or_sem.at[0, half])
+        wait(erecv.at[half], or_sem.at[1, half])
+        acc[OTHER, rows] = precv[rows].astype(F32)
+        both = erecv[half].astype(F32)
+        edge[half * QUART : half * QUART + QUART // 2] = both
+        edge[half * QUART + QUART // 2 : (half + 1) * QUART] = pltpu.roll(both, EDGE, 1)
         for block in range(half * NY // 2, (half + 1) * NY // 2):
-            nat[pl.ds((block * NZL + 1 - zl) * ROWS, ROWS), :] = acc[1, block * ROWS : (block + 1) * ROWS] * gate
+            rows, place = slice(block * ROWS, (block + 1) * ROWS), pl.ds((block * NZL + 1 - zl) * ROWS, ROWS)
+            nat[place, :MAIN] = acc[OTHER, rows]
+            nat[place, MAIN:] = edge[rows]
         for block in ((0, 1, 2), (3, 4, 5, 6))[half]:
             tokens = slice(block * 128, (block + 1) * 128)
-            out_ref[0, :, tokens] = (resv[0, :, tokens].astype(F32) + nat[tokens, :].T).astype(BF16)
+            made = nat[tokens, :].T
+            for at, part in ((main_at, made[:MAIN]), (edge_at, made[MAIN : MAIN + EDGE])):
+                mixed = resv[0, at, tokens].astype(F32) + gate_ref[at, :] * part
+                out_ref[0, at, tokens] = mixed.astype(BF16)
     for half in range(2):
-        wait(psend.at[half * QUART : (half + 1) * QUART], os_sem.at[half])
+        wait(psend.at[half * QUART : (half + 1) * QUART], os_sem.at[0, half])
+        wait(esend.at[half], os_sem.at[1, half])
 
 
 def local(queries, keys, values, residual, wo_values, wo_exponents, modulation, expert_choice, step_index, lengths):
@@ -473,26 +509,26 @@
             pltpu.SMEM((CLIPS,), jnp.int32),
             pltpu.VMEM((3, ROWS, HEADS * HEAD_DIM), BF16),
             pltpu.VMEM((3, NZL, NY, ROWS, 3 * HEAD_DIM), BF16),
-            pltpu.VMEM((3, ROWS, 3 * HEAD_DIM), BF16),
-            pltpu.VMEM((NZL, 2, NZH, 2 * NX * DEPTH, COLS), BF16),
+            pltpu.VMEM((NZL, NZH, 2 * NX * DEPTH, PACK), BF16),
             pltpu.VMEM((2, DEPTH, COLS), BF16),
-            pltpu.VMEM((NZL, NZH, 2 * NX * DEPTH, COLS), BF16),
-            pltpu.VMEM((NX, NZL, NZH, DEPTH, COLS), BF16),
+            pltpu.VMEM((NZH, 2 * NX * DEPTH, PACK), BF16),
+            pltpu.VMEM((NX, NZH, DEPTH, PACK), BF16),
             pltpu.VMEM((NY, HALF, 3 * HEAD_DIM), BF16),
-            pltpu.VMEM((2, HALF, COLS), F32),
-            pltpu.VMEM((HALF, COLS), BF16),
-            pltpu.VMEM((HALF, COLS), BF16),
+            pltpu.VMEM((2, HALF, MAIN), F32),
+            pltpu.VMEM((HALF, 2 * EDGE), F32),
+            pltpu.VMEM((HALF, MAIN), BF16),
+            pltpu.VMEM((HALF, MAIN), BF16),
+            pltpu.VMEM((2, QUART // 2, 2 * EDGE), BF16),
+            pltpu.VMEM((2, QUART // 2, 2 * EDGE), BF16),
             pltpu.VMEM((1, COLS, SEQ), BF16),
-            pltpu.VMEM((SEQ, COLS), F32),
+            pltpu.VMEM((SEQ, MAIN + 2 * EDGE), F32),
             pltpu.VMEM((2, HEADS, COLS), F32),
             pltpu.VMEM((1, SEQ), F32),
-            pltpu.VMEM((1, COLS), F32),
+            pltpu.VMEM((COLS, 128), F32),
             dma((6,)),
             dma((6,)),
             dma((2, NY)),
             dma((2, NY)),
-            dma((2,)),
-            dma((2,)),
             dma((2, NY)),
             dma((2, NY)),
             dma((2, NZ)),
@@ -505,8 +541,8 @@
             dma((NX,)),
             dma((2, NY // 2, 5)),
             dma((2, NY // 2, 5)),
-            dma((2,)),
-            dma((2,)),
+            dma((2, 2)),
+            dma((2, 2)),
         ],
         compiler_params=pltpu.CompilerParams(
             collective_id=0, has_side_effects=True, vmem_limit_bytes=62 * 2**20

time: 77.6 us -> 76.1 us (0.981)
  the two profiles are of different devices: /device:TPU:8 before, /device:TPU:6 now
where the time goes in v2:
time: 76.1 us; the launch traced here: 75.8 us
  Pallas kernels  74.9 us (98%)
  local copies, waits for them, and re-layouts  0.81 us (1%)
    pallas_call x1, Pallas kernels, local(): pl.pallas_call(kernel, out_shape=pltpu.VMEM((1, COLS, SEQ), BF16), in_spe...  74.9 us

profile of v2, /device:TPU:6, one launch (start us, length us, event | category | flops | bytes accessed | tf_op | source)
XLA Modules:
  0.0 75.8 jit_solution(6258309806743142796)
XLA Ops:
  0.0 74.9 %shard_map.109 = bf16[1,320,896]{2,1,0:T(8,128)(2,1)S(1)} custom-call(bf16[1,56,2560]{2,1,0:T(8,128)(2,1)} %q_ref.1, bf16[1,56,2560]{2,1,0:T(8,128)(2,1)} %k_ref.1, bf16[1,56,2560]{2,1,0:T(8,128)(2,1)} %v_ref.1, bf16[1,320,896]{2,1,0:T(8,128)(2,1)} %bitcast.4, bf16[2,80,320]{2,1,0:T(8,128)(2,1)} %wo_ref.1, s32[20,2,40]{2,1,0:T(2,128)} %bitcast.5, ...), custom_call_target="tpu_custom_call" | custom-call | flops 2000000000 | bytes 3000000 | tf_op jit(solution)/shard_map/pallas_call | solution.py:498
  74.9 0.8 %copy.13 = bf16[1,896,320]{1,2,0:T(8,128)(2,1)} copy(bf16[1,896,320]{1,2,0:T(8,128)(2,1)S(1)} %bitcast.3) | data formatting | bytes 1146880

commit v3 on v2

--- a/solution.py
+++ b/solution.py
@@ -327,28 +327,31 @@
 
             lax.fori_loop(0, 2, one, 0)
 
+        order = (4, 3, 5, 2, 6, 1, 7)
         send(own_w, own_w, zs_sem.at[0, 0], zr_sem.at[1], z_next)
         send(own_w, own_w, zs_sem.at[1, 0], zr_sem.at[NZ - 1], z_prev)
         for j in range(3):
             wait(pre.at[j], loc_sem.at[j])
-        for d in (4, 3, 5, 2, 6, 1, 7):
+        own_kv(0)
+        for d in order:
             a2a(d, 0)
-        own_kv(0)
         send(own_w, own_w, xs_sem.at[0, 0], xr_sem.at[0, 0], x_next)
         send(own_w, own_w, xs_sem.at[1, 0], xr_sem.at[1, 0], x_prev)
         start = pl.multiple_of(((y // 2) * 5 + (0 if n == 3 else 3)) * HEAD_DIM, HEAD_DIM)
         own_block = qkv.at[:, zl, y, :, pl.ds(0, n * HEAD_DIM)]
         pltpu.make_async_copy(pre.at[:, :, pl.ds(start, n * HEAD_DIM)], own_block, loc_sem.at[5]).start()
         tables()
-        for d in (4, 3, 5):
+        own_kv(1)
+        for d in order[:3]:
             a2a(d, 1)
         z_tick(1)
         z_tick(7)
+        for d in order[:3]:
+            kv_tick(d, 0)
+        for d in order[3:]:
+            a2a(d, 1)
         x_tick(0)
-        for d in (2, 6, 1, 7):
-            a2a(d, 1)
-        own_kv(1)
-        for d in (1, 7, 2, 6, 3, 5, 4):
+        for d in order[3:]:
             kv_tick(d, 0)
         z_tick(2)
         z_tick(6)
@@ -360,18 +363,18 @@
             attend(0, half, keys, values)
         ring_send(1, 0, 0, y)
         ring_send(1, 1, 0, y)
+        for d in order[:2]:
+            kv_tick(d, 1)
         x_tick(1)
         x_tick(7)
+        for d in order[2:4]:
+            kv_tick(d, 1)
         z_tick(3)
         z_tick(5)
-        kv_tick(1, 1)
-        kv_tick(7, 1)
-        kv_tick(2, 1)
-        kv_tick(6, 1)
+        for d in order[4:6]:
+            kv_tick(d, 1)
         z_tick(4)
-        kv_tick(3, 1)
-        kv_tick(5, 1)
-        kv_tick(4, 1)
+        kv_tick(order[6], 1)
         x_tick(2)
         x_tick(6)
         die_push(x, 0)

time: 76.1 us -> 74.9 us (0.984)
  Pallas kernels: 74.9 us -> 73.9 us
    pallas_call x1, Pallas kernels: 74.9 us -> 73.9 us  [local(): pl.pallas_call(kernel, out_shape=pltpu.VMEM((1, COLS, SEQ), BF16), in_spe...]
where the time goes in v3:
time: 74.9 us; the launch traced here: 74.7 us
  Pallas kernels  73.9 us (99%)
  local copies, waits for them, and re-layouts  0.81 us (1%)
    pallas_call x1, Pallas kernels, local(): pl.pallas_call(kernel, out_shape=pltpu.VMEM((1, COLS, SEQ), BF16), in_spe...  73.9 us

profile of v3, /device:TPU:6, one launch (start us, length us, event | category | flops | bytes accessed | tf_op | source)
XLA Modules:
  0.0 74.7 jit_solution(15050457461004677697)
XLA Ops:
  0.0 73.9 %shard_map.109 = bf16[1,320,896]{2,1,0:T(8,128)(2,1)S(1)} custom-call(bf16[1,56,2560]{2,1,0:T(8,128)(2,1)} %q_ref.1, bf16[1,56,2560]{2,1,0:T(8,128)(2,1)} %k_ref.1, bf16[1,56,2560]{2,1,0:T(8,128)(2,1)} %v_ref.1, bf16[1,320,896]{2,1,0:T(8,128)(2,1)} %bitcast.4, bf16[2,80,320]{2,1,0:T(8,128)(2,1)} %wo_ref.1, s32[20,2,40]{2,1,0:T(2,128)} %bitcast.5, ...), custom_call_target="tpu_custom_call" | custom-call | flops 2000000000 | bytes 3000000 | tf_op jit(solution)/shard_map/pallas_call | solution.py:501
  73.9 0.8 %copy.13 = bf16[1,896,320]{1,2,0:T(8,128)(2,1)} copy(bf16[1,896,320]{1,2,0:T(8,128)(2,1)S(1)} %bitcast.3) | data formatting | bytes 1146880

commit v4 on v3

--- a/solution.py
+++ b/solution.py
@@ -131,11 +131,11 @@
         return wbuf.at[lax.rem(zz, NZL), zz // NZL, pl.ds((xx * 2 + c) * DEPTH, DEPTH), :]
 
     def lanes(phase, n):
-        return pl.ds(0, HEAD_DIM) if phase == 0 else pl.ds(HEAD_DIM, (n - 1) * HEAD_DIM)
+        return pl.ds(0, (n - 1) * HEAD_DIM) if phase == 0 else pl.ds((n - 1) * HEAD_DIM, HEAD_DIM)
 
     def columns(yy, phase, n):
-        first = (yy // 2) * 5 + (0 if n == 3 else 3) + phase
-        return pl.ds(pl.multiple_of(first * HEAD_DIM, HEAD_DIM), HEAD_DIM if phase == 0 else (n - 1) * HEAD_DIM)
+        first = (yy // 2) * 5 + (0 if n == 3 else 3) + phase * (n - 1)
+        return pl.ds(pl.multiple_of(first * HEAD_DIM, HEAD_DIM), (n - 1) * HEAD_DIM if phase == 0 else HEAD_DIM)
 
     small = (
         (exps_hbm, exps_ref),
@@ -274,37 +274,38 @@
             summed = jnp.dot(probs.astype(BF16), values, preferred_element_type=F32)
             attm[y, half * QUART : (half + 1) * QUART, j * HEAD_DIM : (j + 1) * HEAD_DIM] = (summed / total).astype(BF16)
 
+        def kinds(count):
+            return (0, 1, 2, 3) if count == 3 else (0, 2, 3)
+
+        def last_kinds(direction, count):
+            return ((0, 2), (1, 3))[direction] if count == 3 else ((0,), (2, 3))[direction]
+
         def region(yy, kind, count):
-            if kind == 0:
-                return attm.at[yy, :, pl.ds(0, HEAD_DIM)]
-            if kind in (1, 2):
-                return attm.at[yy, pl.ds((kind - 1) * QUART, QUART), pl.ds(HEAD_DIM, (count - 1) * HEAD_DIM)]
-            return attm.at[yy, pl.ds(0, QUART), pl.ds((kind - 2) * HEAD_DIM, HEAD_DIM)]
+            if kind < 2:
+                return attm.at[yy, :, pl.ds(kind * HEAD_DIM, HEAD_DIM)]
+            return attm.at[yy, pl.ds((kind - 2) * QUART, QUART), pl.ds((count - 1) * HEAD_DIM, HEAD_DIM)]
 
         def ring_send(t, direction, kind, yy):
             block = region(yy, kind, heads(t - 1))
             sems = gs_sem.at[direction, t - 1, kind], gr_sem.at[direction, t - 1, kind]
             send(block, block, *sems, (y_next, y_prev)[direction])
 
+        def ring_start(kind):
+            for direction in range(2):
+                ring_send(1, direction, kind, y)
+
         def ring_wait(t, direction, kind):
             yy = mod(y - t if direction == 0 else y + t, NY)
             wait(region(yy, kind, heads(t)), gr_sem.at[direction, t - 1, kind])
             return yy
 
         def ring_tick(t, kind):
+            if kind not in kinds(heads(t)):
+                return
             for direction in range(2):
                 yy = ring_wait(t, direction, kind)
-                if t < NY // 2 - 1:
+                if t < NY // 2 - 1 or kind in last_kinds(direction, heads(t)):
                     ring_send(t + 1, direction, kind, yy)
-                else:
-                    for last_kind in last_kinds(direction, heads(t)):
-                        if last_kind == kind or (kind == 1 and last_kind in (3, 4)):
-                            ring_send(t + 1, direction, last_kind, yy)
-
-        def last_kinds(direction, count):
-            if direction == 1:
-                return (3, 2)
-            return (0, 4) if count == 3 else (0,)
 
         def project(yy, count, part, rows=slice(0, HALF), fresh=False):
             first = 0 if count == 3 else 3 * HEAD_DIM
@@ -351,62 +352,61 @@
         for d in order[3:]:
             a2a(d, 1)
         x_tick(0)
-        for d in order[3:]:
-            kv_tick(d, 0)
         z_tick(2)
         z_tick(6)
+        for d in order[3:5]:
+            kv_tick(d, 0)
+        x_tick(1)
+        x_tick(7)
+        for d in order[5:]:
+            kv_tick(d, 0)
+        z_tick(3)
+        z_tick(5)
 
         wait(own_block, loc_sem.at[5])
         kv_done(0)
-        keys, values = head_rows(1, 0), head_rows(2, 0)
-        for half in range(2):
-            attend(0, half, keys, values)
-        ring_send(1, 0, 0, y)
-        ring_send(1, 1, 0, y)
-        for d in order[:2]:
+        for j in range(n - 1):
+            keys, values = head_rows(1, j), head_rows(2, j)
+            for half in range(2):
+                attend(j, half, keys, values)
+            ring_start(j)
+            for d in order[:2] if j == 0 else order[2:4]:
+                kv_tick(d, 1)
+            if j == 0:
+                z_tick(4)
+        for d in order[2 * (n - 1) :]:
             kv_tick(d, 1)
-        x_tick(1)
-        x_tick(7)
-        for d in order[2:4]:
-            kv_tick(d, 1)
-        z_tick(3)
-        z_tick(5)
-        for d in order[4:6]:
-            kv_tick(d, 1)
-        z_tick(4)
-        kv_tick(order[6], 1)
         x_tick(2)
         x_tick(6)
+        ring_tick(1, 0)
         die_push(x, 0)
-        ring_tick(1, 0)
 
         kv_done(1)
-        pairs = {j: (head_rows(1, j), head_rows(2, j)) for j in range(1, n)}
-        for j in range(1, n):
-            attend(j, 0, *pairs[j])
-        ring_send(1, 0, 1, y)
-        ring_send(1, 1, 1, y)
+        keys, values = head_rows(1, n - 1), head_rows(2, n - 1)
+        attend(n - 1, 0, keys, values)
+        ring_start(2)
+        ring_tick(1, 1)
+        attend(n - 1, 1, keys, values)
+        ring_start(3)
         ring_tick(2, 0)
         x_tick(3)
         x_tick(5)
-        for j in range(1, n):
-            attend(j, 1, *pairs[j])
-        ring_send(1, 0, 2, y)
-        ring_send(1, 1, 2, y)
-        ring_tick(1, 1)
+        ring_tick(2, 1)
+        ring_tick(1, 2)
+        ring_tick(1, 3)
         x_tick(4)
-        ring_tick(3, 0)
-        ring_tick(1, 2)
         die_push(mod(x - 1, NX), 1)
         die_push(mod(x + 1, NX), 2)
-        ring_tick(2, 1)
+        ring_tick(3, 0)
         ring_tick(2, 2)
+        ring_tick(2, 3)
+        ring_tick(3, 1)
         far = mod(x + 2, NX)
         for d in range(NZ):
             wait(wslot(mod(z - d, NZ), far), rr_sem.at[d])
         die_push(far, 3)
-        ring_tick(3, 1)
         ring_tick(3, 2)
+        ring_tick(3, 3)
         for index, xx in enumerate((x, mod(x - 1, NX), mod(x + 1, NX), far)):
             wait(wch.at[:, pl.ds((xx * 2 + 1 - c) * DEPTH, DEPTH), :], dr_sem.at[index])
         project(y, n, OTHER, fresh=True)
@@ -419,10 +419,9 @@
         last = mod(y + NY // 2, NY)
         turned = lax.rem(expert_ref[rep] + zl, 2) * EDGE
         left = lax.broadcasted_iota(jnp.int32, (QUART // 2, 2 * EDGE), 1) < EDGE
-        for kind in last_kinds(0, n):
-            ring_wait(NY // 2, 0, kind)
         for half in range(2):
-            ring_wait(NY // 2, 1, (3, 2)[half])
+            for kind in ((0, 1, 2) if n == 3 else (0, 2)) if half == 0 else (3,):
+                ring_wait(NY // 2, 0 if kind in last_kinds(0, n) else 1, kind)
             rows = slice(half * QUART, (half + 1) * QUART)
             project(last, n, OTHER, rows)
             psend[rows] = acc[OTHER, rows].astype(BF16)
@@ -445,7 +444,7 @@
                 wait(qkv.at[pl.ds(1, 2), zl, source, :, lanes(phase, n)], ks_sem.at[phase, source])
         for t in range(1, NY // 2 + 1):
             for direction in range(2):
-                for kind in (0, 1, 2) if t < NY // 2 else last_kinds(direction, heads(t - 1)):
+                for kind in kinds(heads(t - 1)) if t < NY // 2 else last_kinds(direction, heads(t - 1)):
                     wait(region(y, kind, heads(t - 1)), gs_sem.at[direction, t - 1, kind])
 
     pl.when(lax.rem(y, 2) == 0)(lambda: run(3))

time: 74.9 us -> 73.7 us (0.984)
  Pallas kernels: 73.9 us -> 72.7 us
    pallas_call x1, Pallas kernels: 73.9 us -> 72.7 us  [local(): pl.pallas_call(kernel, out_shape=pltpu.VMEM((1, COLS, SEQ), BF16), in_spe...]
where the time goes in v4:
time: 73.7 us; the launch traced here: 73.6 us
  Pallas kernels  72.7 us (99%)
  local copies, waits for them, and re-layouts  0.81 us (1%)
    pallas_call x1, Pallas kernels, local(): pl.pallas_call(kernel, out_shape=pltpu.VMEM((1, COLS, SEQ), BF16), in_spe...  72.7 us

profile of v4, /device:TPU:6, one launch (start us, length us, event | category | flops | bytes accessed | tf_op | source)
XLA Modules:
  0.0 73.6 jit_solution(9738122108775886553)
XLA Ops:
  0.0 72.7 %shard_map.109 = bf16[1,320,896]{2,1,0:T(8,128)(2,1)S(1)} custom-call(bf16[1,56,2560]{2,1,0:T(8,128)(2,1)} %q_ref.1, bf16[1,56,2560]{2,1,0:T(8,128)(2,1)} %k_ref.1, bf16[1,56,2560]{2,1,0:T(8,128)(2,1)} %v_ref.1, bf16[1,320,896]{2,1,0:T(8,128)(2,1)} %bitcast.4, bf16[2,80,320]{2,1,0:T(8,128)(2,1)} %wo_ref.1, s32[20,2,40]{2,1,0:T(2,128)} %bitcast.5, ...), custom_call_target="tpu_custom_call" | custom-call | flops 2000000000 | bytes 3000000 | tf_op jit(solution)/shard_map/pallas_call | solution.py:500
  72.8 0.8 %copy.13 = bf16[1,896,320]{1,2,0:T(8,128)(2,1)} copy(bf16[1,896,320]{1,2,0:T(8,128)(2,1)S(1)} %bitcast.3) | data formatting | bytes 1146880

commit v5 on v4

--- a/solution.py
+++ b/solution.py
@@ -351,14 +351,9 @@
             kv_tick(d, 0)
         for d in order[3:]:
             a2a(d, 1)
-        x_tick(0)
         z_tick(2)
         z_tick(6)
-        for d in order[3:5]:
-            kv_tick(d, 0)
-        x_tick(1)
-        x_tick(7)
-        for d in order[5:]:
+        for d in order[3:]:
             kv_tick(d, 0)
         z_tick(3)
         z_tick(5)
@@ -374,6 +369,9 @@
                 kv_tick(d, 1)
             if j == 0:
                 z_tick(4)
+                x_tick(0)
+                x_tick(1)
+                x_tick(7)
         for d in order[2 * (n - 1) :]:
             kv_tick(d, 1)
         x_tick(2)
@@ -395,6 +393,11 @@
         ring_tick(1, 2)
         ring_tick(1, 3)
         x_tick(4)
+        for phase in range(2):
+            for d in range(1, NY):
+                wait(qkv.at[:, zl, y, :, lanes(phase, heads(d))], as_sem.at[phase, d])
+            for source in range(NY):
+                wait(qkv.at[pl.ds(1, 2), zl, source, :, lanes(phase, n)], ks_sem.at[phase, source])
         die_push(mod(x - 1, NX), 1)
         die_push(mod(x + 1, NX), 2)
         ring_tick(3, 0)
@@ -437,11 +440,6 @@
         project_two(3, 2, OWN)
         project(last, n, OWN)
 
-        for phase in range(2):
-            for d in range(1, NY):
-                wait(qkv.at[:, zl, y, :, lanes(phase, heads(d))], as_sem.at[phase, d])
-            for source in range(NY):
-                wait(qkv.at[pl.ds(1, 2), zl, source, :, lanes(phase, n)], ks_sem.at[phase, source])
         for t in range(1, NY // 2 + 1):
             for direction in range(2):
                 for kind in kinds(heads(t - 1)) if t < NY // 2 else last_kinds(direction, heads(t - 1)):

time: 73.7 us -> 73.7 us (level)
  no operation moved by 1% of the time
where the time goes in v5:
time: 73.7 us; the launch traced here: 73.6 us
  Pallas kernels  72.7 us (99%)
  local copies, waits for them, and re-layouts  0.81 us (1%)
    pallas_call x1, Pallas kernels, local(): pl.pallas_call(kernel, out_shape=pltpu.VMEM((1, COLS, SEQ), BF16), in_spe...  72.7 us

profile of v5, /device:TPU:6, one launch (start us, length us, event | category | flops | bytes accessed | tf_op | source)
XLA Modules:
  0.0 73.6 jit_solution(9657986071628716574)
XLA Ops:
  0.0 72.7 %shard_map.109 = bf16[1,320,896]{2,1,0:T(8,128)(2,1)S(1)} custom-call(bf16[1,56,2560]{2,1,0:T(8,128)(2,1)} %q_ref.1, bf16[1,56,2560]{2,1,0:T(8,128)(2,1)} %k_ref.1, bf16[1,56,2560]{2,1,0:T(8,128)(2,1)} %v_ref.1, bf16[1,320,896]{2,1,0:T(8,128)(2,1)} %bitcast.4, bf16[2,80,320]{2,1,0:T(8,128)(2,1)} %wo_ref.1, s32[20,2,40]{2,1,0:T(2,128)} %bitcast.5, ...), custom_call_target="tpu_custom_call" | custom-call | flops 2000000000 | bytes 3000000 | tf_op jit(solution)/shard_map/pallas_call | solution.py:498
  72.8 0.8 %copy.13 = bf16[1,896,320]{1,2,0:T(8,128)(2,1)} copy(bf16[1,896,320]{1,2,0:T(8,128)(2,1)S(1)} %bitcast.3) | data formatting | bytes 1146880

commit v6 on v5

--- a/solution.py
+++ b/solution.py
@@ -160,29 +160,31 @@
     pltpu.make_async_copy(res_ref, resv, loc_sem.at[4]).start()
     own_w = wslot(z, x)
 
-    for index, (source, target) in enumerate(small):
-        pltpu.make_async_copy(source, target, small_sem.at[index]).wait()
-    for choice in range(2):
-        powers = (jnp.left_shift(jnp.ones((HEADS, D // 128), jnp.int32), exps_ref[:, choice, :] + 1).astype(F32) * 0.5).astype(BF16)
-        column = seq * COLS + lax.broadcasted_iota(jnp.int32, (D // 128, COLS), 1)
-        hot = (column // 128 == lax.broadcasted_iota(jnp.int32, (D // 128, COLS), 0)).astype(F32).astype(BF16)
-        stab[choice] = jnp.dot(powers, hot, preferred_element_type=F32)
-    wait(wo_rows, loc_sem.at[3])
-    for choice in range(2):
-        for piece in range(DEPTH // 16):
-            head = (rep * DEPTH + piece * 16) // HEAD_DIM
-            rows = wo_rows[choice, piece * 16 : (piece + 1) * 16, :].astype(F32) * stab[choice, pl.ds(head, 1), :]
-            wo_rows[choice, piece * 16 : (piece + 1) * 16, :] = rows.astype(BF16)
-    packed = jnp.zeros((DEPTH, PACK), F32)
-    origin = lax.broadcasted_iota(jnp.int32, (COLS, PACK), 0)
-    lane = lax.broadcasted_iota(jnp.int32, (COLS, PACK), 1)
-    for choice in range(2):
-        low = jnp.where(origin < MAIN, choice * MAIN + origin, 2 * MAIN + choice * EDGE + origin - MAIN)
-        high = jnp.where(origin < EDGE, 2 * MAIN + (1 - choice) * EDGE + origin, choice * MAIN + origin - EDGE)
-        hot = (lane == jnp.where(zl == 0, low, high)).astype(F32).astype(BF16)
-        packed += jnp.dot(wo_rows[choice], hot, preferred_element_type=F32)
-    wbuf[zl, zh, pl.ds(pl.multiple_of((x * 2 + c) * DEPTH, 16), DEPTH), :] = packed.astype(BF16)
     pl.semaphore_wait(barrier, 12)
+
+    def pack_own():
+        for index, (source, target) in enumerate(small):
+            pltpu.make_async_copy(source, target, small_sem.at[index]).wait()
+        for choice in range(2):
+            powers = (jnp.left_shift(jnp.ones((HEADS, D // 128), jnp.int32), exps_ref[:, choice, :] + 1).astype(F32) * 0.5).astype(BF16)
+            column = seq * COLS + lax.broadcasted_iota(jnp.int32, (D // 128, COLS), 1)
+            hot = (column // 128 == lax.broadcasted_iota(jnp.int32, (D // 128, COLS), 0)).astype(F32).astype(BF16)
+            stab[choice] = jnp.dot(powers, hot, preferred_element_type=F32)
+        wait(wo_rows, loc_sem.at[3])
+        for choice in range(2):
+            for piece in range(DEPTH // 16):
+                head = (rep * DEPTH + piece * 16) // HEAD_DIM
+                rows = wo_rows[choice, piece * 16 : (piece + 1) * 16, :].astype(F32) * stab[choice, pl.ds(head, 1), :]
+                wo_rows[choice, piece * 16 : (piece + 1) * 16, :] = rows.astype(BF16)
+        packed = jnp.zeros((DEPTH, PACK), F32)
+        origin = lax.broadcasted_iota(jnp.int32, (COLS, PACK), 0)
+        lane = lax.broadcasted_iota(jnp.int32, (COLS, PACK), 1)
+        for choice in range(2):
+            low = jnp.where(origin < MAIN, choice * MAIN + origin, 2 * MAIN + choice * EDGE + origin - MAIN)
+            high = jnp.where(origin < EDGE, 2 * MAIN + (1 - choice) * EDGE + origin, choice * MAIN + origin - EDGE)
+            hot = (lane == jnp.where(zl == 0, low, high)).astype(F32).astype(BF16)
+            packed += jnp.dot(wo_rows[choice], hot, preferred_element_type=F32)
+        wbuf[zl, zh, pl.ds(pl.multiple_of((x * 2 + c) * DEPTH, 16), DEPTH), :] = packed.astype(BF16)
 
     def tables():
         flat = lax.broadcasted_iota(jnp.int32, (1, SEQ), 1)
@@ -329,13 +331,14 @@
             lax.fori_loop(0, 2, one, 0)
 
         order = (4, 3, 5, 2, 6, 1, 7)
-        send(own_w, own_w, zs_sem.at[0, 0], zr_sem.at[1], z_next)
-        send(own_w, own_w, zs_sem.at[1, 0], zr_sem.at[NZ - 1], z_prev)
         for j in range(3):
             wait(pre.at[j], loc_sem.at[j])
         own_kv(0)
         for d in order:
             a2a(d, 0)
+        pack_own()
+        send(own_w, own_w, zs_sem.at[0, 0], zr_sem.at[1], z_next)
+        send(own_w, own_w, zs_sem.at[1, 0], zr_sem.at[NZ - 1], z_prev)
         send(own_w, own_w, xs_sem.at[0, 0], xr_sem.at[0, 0], x_next)
         send(own_w, own_w, xs_sem.at[1, 0], xr_sem.at[1, 0], x_prev)
         start = pl.multiple_of(((y // 2) * 5 + (0 if n == 3 else 3)) * HEAD_DIM, HEAD_DIM)
@@ -391,23 +394,23 @@
         x_tick(5)
         ring_tick(2, 1)
         ring_tick(1, 2)
+        x_tick(4)
         ring_tick(1, 3)
-        x_tick(4)
+        ring_tick(3, 0)
+        ring_tick(3, 1)
+        die_push(mod(x - 1, NX), 1)
+        die_push(mod(x + 1, NX), 2)
+        ring_tick(2, 2)
+        ring_tick(2, 3)
+        far = mod(x + 2, NX)
+        for d in range(NZ):
+            wait(wslot(mod(z - d, NZ), far), rr_sem.at[d])
+        die_push(far, 3)
         for phase in range(2):
             for d in range(1, NY):
                 wait(qkv.at[:, zl, y, :, lanes(phase, heads(d))], as_sem.at[phase, d])
             for source in range(NY):
                 wait(qkv.at[pl.ds(1, 2), zl, source, :, lanes(phase, n)], ks_sem.at[phase, source])
-        die_push(mod(x - 1, NX), 1)
-        die_push(mod(x + 1, NX), 2)
-        ring_tick(3, 0)
-        ring_tick(2, 2)
-        ring_tick(2, 3)
-        ring_tick(3, 1)
-        far = mod(x + 2, NX)
-        for d in range(NZ):
-            wait(wslot(mod(z - d, NZ), far), rr_sem.at[d])
-        die_push(far, 3)
         ring_tick(3, 2)
         ring_tick(3, 3)
         for index, xx in enumerate((x, mod(x - 1, NX), mod(x + 1, NX), far)):

time: 73.7 us -> 73.7 us (level)
  no operation moved by 1% of the time
where the time goes in v6:
time: 73.7 us; the launch traced here: 73.6 us
  Pallas kernels  72.7 us (99%)
  local copies, waits for them, and re-layouts  0.81 us (1%)
    pallas_call x1, Pallas kernels, local(): pl.pallas_call(kernel, out_shape=pltpu.VMEM((1, COLS, SEQ), BF16), in_spe...  72.7 us

profile of v6, /device:TPU:6, one launch (start us, length us, event | category | flops | bytes accessed | tf_op | source)
XLA Modules:
  0.0 73.6 jit_solution(8402983732316645436)
XLA Ops:
  0.0 72.7 %shard_map.109 = bf16[1,320,896]{2,1,0:T(8,128)(2,1)S(1)} custom-call(bf16[1,56,2560]{2,1,0:T(8,128)(2,1)} %q_ref.1, bf16[1,56,2560]{2,1,0:T(8,128)(2,1)} %k_ref.1, bf16[1,56,2560]{2,1,0:T(8,128)(2,1)} %v_ref.1, bf16[1,320,896]{2,1,0:T(8,128)(2,1)} %bitcast.4, bf16[2,80,320]{2,1,0:T(8,128)(2,1)} %wo_ref.1, s32[20,2,40]{2,1,0:T(2,128)} %bitcast.5, ...), custom_call_target="tpu_custom_call" | custom-call | flops 2000000000 | bytes 3000000 | tf_op jit(solution)/shard_map/pallas_call | solution.py:501
  72.8 0.8 %copy.13 = bf16[1,896,320]{1,2,0:T(8,128)(2,1)} copy(bf16[1,896,320]{1,2,0:T(8,128)(2,1)S(1)} %bitcast.3) | data formatting | bytes 1146880

commit v7 on v6

--- a/solution.py
+++ b/solution.py
@@ -60,6 +60,7 @@
     len_ref,
     pre,
     qkv,
+    stage,
     wbuf,
     wo_rows,
     wch,
@@ -80,6 +81,8 @@
     small_sem,
     as_sem,
     ar_sem,
+    sr_sem,
+    fs_sem,
     ks_sem,
     kr_sem,
     zs_sem,
@@ -198,6 +201,9 @@
         gate = mod_ref[pl.ds(expert_ref[rep], 1), :] + feature
         gate_ref[...] = jnp.broadcast_to(gate, (128, COLS)).T
 
+    twice = 2 - 4 * c
+    mid_to, mid_from = mod(y + twice, NY), mod(y - twice, NY)
+
     def run(n):
         def heads(d):
             return n if d % 2 == 0 else 5 - n
@@ -206,12 +212,21 @@
             to = mod(y + d, NY)
             cut = lanes(phase, heads(d))
             source = pre.at[:, :, columns(to, phase, heads(d))]
-            send(source, qkv.at[:, zl, y, :, cut], as_sem.at[phase, d], ar_sem.at[phase, d], dev_y(to))
+            if d == NY // 2:
+                send(source, stage.at[:, :, cut], as_sem.at[phase, d], sr_sem.at[phase], dev_y(mid_to))
+            else:
+                send(source, qkv.at[:, zl, y, :, cut], as_sem.at[phase, d], ar_sem.at[phase, d], dev_y(to))
 
         def own_kv(phase):
             source = pre.at[pl.ds(1, 2), :, columns(y, phase, n)]
             target = qkv.at[pl.ds(1, 2), zl, y, :, lanes(phase, n)]
             send(source, target, ks_sem.at[phase, y], kr_sem.at[phase, y], partner)
+
+        def mid_tick(phase):
+            block = stage.at[:, :, lanes(phase, n)]
+            wait(block, sr_sem.at[phase])
+            target = qkv.at[:, zl, mid_from, :, lanes(phase, n)]
+            send(block, target, fs_sem.at[phase], ar_sem.at[phase, NY // 2], dev_y(mid_to))
 
         def kv_tick(d, phase):
             source = mod(y - d, NY)
@@ -330,7 +345,7 @@
 
             lax.fori_loop(0, 2, one, 0)
 
-        order = (4, 3, 5, 2, 6, 1, 7)
+        order, served = (4, 3, 5, 2, 6, 1, 7), (3, 5, 2, 6, 1, 7, 4)
         for j in range(3):
             wait(pre.at[j], loc_sem.at[j])
         own_kv(0)
@@ -345,19 +360,21 @@
         own_block = qkv.at[:, zl, y, :, pl.ds(0, n * HEAD_DIM)]
         pltpu.make_async_copy(pre.at[:, :, pl.ds(start, n * HEAD_DIM)], own_block, loc_sem.at[5]).start()
         tables()
+        mid_tick(0)
         own_kv(1)
         for d in order[:3]:
             a2a(d, 1)
         z_tick(1)
         z_tick(7)
-        for d in order[:3]:
+        for d in served[:3]:
             kv_tick(d, 0)
         for d in order[3:]:
             a2a(d, 1)
         z_tick(2)
         z_tick(6)
-        for d in order[3:]:
+        for d in served[3:]:
             kv_tick(d, 0)
+        mid_tick(1)
         z_tick(3)
         z_tick(5)
 
@@ -368,14 +385,14 @@
             for half in range(2):
                 attend(j, half, keys, values)
             ring_start(j)
-            for d in order[:2] if j == 0 else order[2:4]:
+            for d in served[:2] if j == 0 else served[2:4]:
                 kv_tick(d, 1)
             if j == 0:
                 z_tick(4)
                 x_tick(0)
                 x_tick(1)
                 x_tick(7)
-        for d in order[2 * (n - 1) :]:
+        for d in served[2 * (n - 1) :]:
             kv_tick(d, 1)
         x_tick(2)
         x_tick(6)
@@ -409,6 +426,7 @@
         for phase in range(2):
             for d in range(1, NY):
                 wait(qkv.at[:, zl, y, :, lanes(phase, heads(d))], as_sem.at[phase, d])
+            wait(stage.at[:, :, lanes(phase, n)], fs_sem.at[phase])
             for source in range(NY):
                 wait(qkv.at[pl.ds(1, 2), zl, source, :, lanes(phase, n)], ks_sem.at[phase, source])
         ring_tick(3, 2)
@@ -512,6 +530,7 @@
             pltpu.SMEM((CLIPS,), jnp.int32),
             pltpu.VMEM((3, ROWS, HEADS * HEAD_DIM), BF16),
             pltpu.VMEM((3, NZL, NY, ROWS, 3 * HEAD_DIM), BF16),
+            pltpu.VMEM((3, ROWS, 3 * HEAD_DIM), BF16),
             pltpu.VMEM((NZL, NZH, 2 * NX * DEPTH, PACK), BF16),
             pltpu.VMEM((2, DEPTH, COLS), BF16),
             pltpu.VMEM((NZH, 2 * NX * DEPTH, PACK), BF16),
@@ -532,6 +551,8 @@
             dma((6,)),
             dma((2, NY)),
             dma((2, NY)),
+            dma((2,)),
+            dma((2,)),
             dma((2, NY)),
             dma((2, NY)),
             dma((2, NZ)),

time: 73.7 us -> 73.8 us (level)
  no operation moved by 1% of the time
where the time goes in v7:
time: 73.8 us; the launch traced here: 73.3 us
  Pallas kernels  72.5 us (98%)
  local copies, waits for them, and re-layouts  0.81 us (1%)
    pallas_call x1, Pallas kernels, local(): pl.pallas_call(kernel, out_shape=pltpu.VMEM((1, COLS, SEQ), BF16), in_spe...  72.5 us

profile of v7, /device:TPU:6, one launch (start us, length us, event | category | flops | bytes accessed | tf_op | source)
XLA Modules:
  0.0 73.3 jit_solution(4715121180857582191)
XLA Ops:
  0.0 72.5 %shard_map.109 = bf16[1,320,896]{2,1,0:T(8,128)(2,1)S(1)} custom-call(bf16[1,56,2560]{2,1,0:T(8,128)(2,1)} %q_ref.1, bf16[1,56,2560]{2,1,0:T(8,128)(2,1)} %k_ref.1, bf16[1,56,2560]{2,1,0:T(8,128)(2,1)} %v_ref.1, bf16[1,320,896]{2,1,0:T(8,128)(2,1)} %bitcast.4, bf16[2,80,320]{2,1,0:T(8,128)(2,1)} %wo_ref.1, s32[20,2,40]{2,1,0:T(2,128)} %bitcast.5, ...), custom_call_target="tpu_custom_call" | custom-call | flops 2000000000 | bytes 3000000 | tf_op jit(solution)/shard_map/pallas_call | solution.py:519
  72.5 0.8 %copy.13 = bf16[1,896,320]{1,2,0:T(8,128)(2,1)} copy(bf16[1,896,320]{1,2,0:T(8,128)(2,1)S(1)} %bitcast.3) | data formatting | bytes 1146880

commit v8 on v6

--- a/solution.py
+++ b/solution.py
@@ -346,14 +346,12 @@
         pltpu.make_async_copy(pre.at[:, :, pl.ds(start, n * HEAD_DIM)], own_block, loc_sem.at[5]).start()
         tables()
         own_kv(1)
-        for d in order[:3]:
+        for d in order:
             a2a(d, 1)
         z_tick(1)
         z_tick(7)
         for d in order[:3]:
             kv_tick(d, 0)
-        for d in order[3:]:
-            a2a(d, 1)
         z_tick(2)
         z_tick(6)
         for d in order[3:]:

time: 73.7 us -> 73.7 us (level)
  no operation moved by 1% of the time
where the time goes in v8:
time: 73.7 us; the launch traced here: 73.6 us
  Pallas kernels  72.8 us (99%)
  local copies, waits for them, and re-layouts  0.81 us (1%)
    pallas_call x1, Pallas kernels, local(): pl.pallas_call(kernel, out_shape=pltpu.VMEM((1, COLS, SEQ), BF16), in_spe...  72.8 us

profile of v8, /device:TPU:6, one launch (start us, length us, event | category | flops | bytes accessed | tf_op | source)
XLA Modules:
  0.0 73.6 jit_solution(14247637967812058507)
XLA Ops:
  0.0 72.8 %shard_map.109 = bf16[1,320,896]{2,1,0:T(8,128)(2,1)S(1)} custom-call(bf16[1,56,2560]{2,1,0:T(8,128)(2,1)} %q_ref.1, bf16[1,56,2560]{2,1,0:T(8,128)(2,1)} %k_ref.1, bf16[1,56,2560]{2,1,0:T(8,128)(2,1)} %v_ref.1, bf16[1,320,896]{2,1,0:T(8,128)(2,1)} %bitcast.4, bf16[2,80,320]{2,1,0:T(8,128)(2,1)} %wo_ref.1, s32[20,2,40]{2,1,0:T(2,128)} %bitcast.5, ...), custom_call_target="tpu_custom_call" | custom-call | flops 2000000000 | bytes 3000000 | tf_op jit(solution)/shard_map/pallas_call | solution.py:499
  72.8 0.8 %copy.13 = bf16[1,896,320]{1,2,0:T(8,128)(2,1)} copy(bf16[1,896,320]{1,2,0:T(8,128)(2,1)S(1)} %bitcast.3) | data formatting | bytes 1146880
